TPU v7x, 512 devices: a whole 4x4x16 slice. The times are simulated.
512 devices in a mesh: pair: 64 (over x_lo, z, core), band: 8 (over y, x_hi).
Axes of the slice: x: 4 (x_hi: 2, x_lo: 2; x = x_hi * 2 + x_lo), y: 4, z: 16, core: 2. Of those that a mesh axis runs over, the one named last changes fastest.
Arguments:
- spectra: bfloat16 [2, 64, 512, 2048], P(None, None, 'pair', 'band'), may hold values from -40 to 40
- validity: int32 [64, 512], P(None, 'pair'), may hold values 0 or 1
Outputs:
- correlations: float32 [7, 512, 8, 128], P(None, 'pair', 'band')
All inputs are finite; a program needn't handle non-finite values. No bound on the sum of `validity` on one device may be relied on, other than what follows from the above.
Results may differ from a plain program's by a relative error of at most 0.004.
Values may be sent and summed in bfloat16 or wider, within the bound.
No kernel may reach another device: no remote copies, remote signals or barrier semaphores. Data moves between devices by JAX's collectives and lax.ppermute only.
A program may use at most 64 MiB of HBM per device.

v0:
```python
import math

import jax
import jax.numpy as jnp
from jax import lax
from jax.sharding import PartitionSpec as P

WIN = 64
ROUNDS = 6
BAND_BINS = 128
LAGS = 128
NBINS = 2048


def passed_along(value, axis, steps):
    count = lax.axis_size(axis)
    pairs = [(source, (source + steps) % count) for source in range(count)]
    return lax.ppermute(value, axis, pairs)


def whiten(spectra, validity):
    values = spectra.astype(jnp.float32)
    magnitude = jnp.sqrt(values[0] * values[0] + values[1] * values[1])
    win_count, station_count, bin_count = magnitude.shape
    grouped = magnitude.reshape(win_count, station_count, bin_count // BAND_BINS, BAND_BINS)
    band_mean = jnp.mean(grouped, axis=-1, keepdims=True)
    factor = jnp.broadcast_to(1.0 / (band_mean + 1e-06), grouped.shape).reshape(
        win_count, station_count, bin_count
    )
    factor = factor * validity.astype(jnp.float32)[:, :, None]
    return (values * factor[None]).astype(jnp.bfloat16)


def lag_table(first_bin, bin_count):
    freq = first_bin + jnp.arange(bin_count, dtype=jnp.int32)
    offsets = jnp.arange(LAGS, dtype=jnp.int32) - LAGS // 2
    wrapped = freq[:, None] * offsets[None, :] % (2 * NBINS)
    phase_arg = math.pi * wrapped.astype(jnp.float32) / NBINS
    return jnp.concatenate([jnp.cos(phase_arg), -jnp.sin(phase_arg)], axis=0)


def body(spectra, validity):
    whitened = whiten(spectra, validity)
    station_count = spectra.shape[2]
    bin_count = spectra.shape[3]
    lag_matrix = lag_table(lax.axis_index("band") * bin_count, bin_count)
    off_diag = 1.0 - jnp.eye(station_count, dtype=jnp.float32)
    win_scale = 1.0 / math.sqrt(WIN)
    bin_scale = 1.0 / math.sqrt(NBINS)
    results = []
    partner = whitened
    for round_no in range(ROUNDS + 1):
        if round_no == 0:
            partner = whitened
        else:
            partner = passed_along(whitened, "pair", -round_no)
        real_part = jnp.einsum(
            "cwpf,cwqf->pqf", whitened, partner, preferred_element_type=jnp.float32
        )
        flipped = jnp.stack([partner[1], -partner[0]])
        imag_part = jnp.einsum(
            "cwpf,cwqf->pqf", whitened, flipped, preferred_element_type=jnp.float32
        )
        real_part = real_part * win_scale
        imag_part = imag_part * win_scale
        if round_no == 0:
            real_part = real_part * off_diag[:, :, None]
            imag_part = imag_part * off_diag[:, :, None]
        joined = jnp.concatenate([real_part, imag_part], axis=-1).reshape(
            station_count * station_count, 2 * bin_count
        )
        lagged = jnp.dot(
            joined, lag_matrix, precision=lax.Precision.HIGHEST, preferred_element_type=jnp.float32
        )
        block_terms = (lagged * bin_scale).reshape(station_count, station_count, LAGS)
        results.append(lax.psum_scatter(block_terms, "band", scatter_dimension=1, tiled=True))
    return jnp.stack(results)


def solution(mesh):
    return jax.shard_map(
        body,
        mesh=mesh,
        in_specs=(P(None, None, "pair", "band"), P(None, "pair")),
        out_specs=P(None, "pair", "band", None),
        check_vma=False,
    )
```

profile of v0, /device:TPU:1, one launch (start us, length us, event | category | flops | bytes accessed | tf_op | source)
XLA Modules:
  0.0 286.7 jit_solution(16745751497572610960)
XLA Ops:
  6.5 2.5 copy.26
  10.2 2.0 copy.30
  12.2 13.8 %collective-permute-start.5 = (bf16[2,64,8,256]{3,2,1,0:T(8,128)(2,1)}, bf16[2,64,8,256]{3,2,1,0:T(8,128)(2,1)}, u32[]{:S(2)}, u32[]{:S(2)}) collective-permute-start(bf16[2,64,8,256]{3,2,1,0:T(8,128)(2,1)} %copy.30), channel_id=1, source_target_pairs={{0,464},{8,472},{16,480},{24,488},{32,496},{40,504},{48,0},{56,8},... | collective-permute-start | bytes 1572872 | tf_op jit(solution)/shard_map/ppermute | solution.py:18
  26.0 5.1 %collective-permute-start.4 = (bf16[2,64,8,256]{3,2,1,0:T(8,128)(2,1)}, bf16[2,64,8,256]{3,2,1,0:T(8,128)(2,1)}, u32[]{:S(2)}, u32[]{:S(2)}) collective-permute-start(bf16[2,64,8,256]{3,2,1,0:T(8,128)(2,1)} %copy.30), channel_id=1, source_target_pairs={{0,472},{8,480},{16,488},{24,496},{32,504},{40,0},{48,8},{56,16},{... | collective-permute-start | bytes 1572872 | tf_op jit(solution)/shard_map/ppermute | solution.py:18
  31.1 3.1 %collective-permute-start.3 = (bf16[2,64,8,256]{3,2,1,0:T(8,128)(2,1)}, bf16[2,64,8,256]{3,2,1,0:T(8,128)(2,1)}, u32[]{:S(2)}, u32[]{:S(2)}) collective-permute-start(bf16[2,64,8,256]{3,2,1,0:T(8,128)(2,1)} %copy.30), channel_id=1, source_target_pairs={{0,480},{8,488},{16,496},{24,504},{32,0},{40,8},{48,16},{56,24},{6... | collective-permute-start | bytes 1572872 | tf_op jit(solution)/shard_map/ppermute | solution.py:18
  34.2 1.9 collective-permute-start.2
  36.1 2.6 collective-permute-start.1
  38.9 0.4 fusion
  39.3 0.5 fusion.1
  40.6 0.6 fusion.73
  41.5 0.6 copy.29
  42.1 23.0 %collective-permute-done.5 = bf16[2,64,8,256]{3,2,1,0:T(8,128)(2,1)} collective-permute-done((bf16[2,64,8,256]{3,2,1,0:T(8,128)(2,1)}, bf16[2,64,8,256]{3,2,1,0:T(8,128)(2,1)}, u32[]{:S(2)}, u32[]{:S(2)}) %collective-permute-start.5) | collective-permute-done | bytes 524320 | tf_op jit(solution)/shard_map/ppermute | solution.py:18
  65.1 5.3 %collective-permute-start = (bf16[2,64,8,256]{3,2,1,0:T(8,128)(2,1)}, bf16[2,64,8,256]{3,2,1,0:T(8,128)(2,1)}, u32[]{:S(2)}, u32[]{:S(2)}) collective-permute-start(bf16[2,64,8,256]{3,2,1,0:T(8,128)(2,1)} %copy.30), channel_id=1, source_target_pairs={{0,504},{8,0},{16,8},{24,16},{32,24},{40,32},{48,40},{56,48},{64,5... | collective-permute-start | bytes 1572872 | tf_op jit(solution)/shard_map/ppermute | solution.py:18
  70.5 2.5 copy.66
  73.0 1.1 fusion.88
  74.1 1.4 fusion.23
  75.5 18.3 %collective-permute-done.4 = bf16[2,64,8,256]{3,2,1,0:T(8,128)(2,1)} collective-permute-done((bf16[2,64,8,256]{3,2,1,0:T(8,128)(2,1)}, bf16[2,64,8,256]{3,2,1,0:T(8,128)(2,1)}, u32[]{:S(2)}, u32[]{:S(2)}) %collective-permute-start.4) | collective-permute-done | bytes 524320 | tf_op jit(solution)/shard_map/ppermute | solution.py:18
  93.7 2.5 copy.59
  96.2 1.2 fusion.89
  97.4 1.5 fusion.19
  98.9 11.6 %collective-permute-done.3 = bf16[2,64,8,256]{3,2,1,0:T(8,128)(2,1)} collective-permute-done((bf16[2,64,8,256]{3,2,1,0:T(8,128)(2,1)}, bf16[2,64,8,256]{3,2,1,0:T(8,128)(2,1)}, u32[]{:S(2)}, u32[]{:S(2)}) %collective-permute-start.3) | collective-permute-done | bytes 524320 | tf_op jit(solution)/shard_map/ppermute | solution.py:18
  110.6 2.5 copy.52
  113.0 1.1 fusion.90
  114.1 1.4 fusion.15
  115.5 12.0 %collective-permute-done.2 = bf16[2,64,8,256]{3,2,1,0:T(8,128)(2,1)} collective-permute-done((bf16[2,64,8,256]{3,2,1,0:T(8,128)(2,1)}, bf16[2,64,8,256]{3,2,1,0:T(8,128)(2,1)}, u32[]{:S(2)}, u32[]{:S(2)}) %collective-permute-start.2) | collective-permute-done | bytes 524320 | tf_op jit(solution)/shard_map/ppermute | solution.py:18
  127.5 2.5 copy.45
  130.0 1.1 fusion.91
  131.2 1.4 fusion.11
  132.5 6.2 %collective-permute-done.1 = bf16[2,64,8,256]{3,2,1,0:T(8,128)(2,1)} collective-permute-done((bf16[2,64,8,256]{3,2,1,0:T(8,128)(2,1)}, bf16[2,64,8,256]{3,2,1,0:T(8,128)(2,1)}, u32[]{:S(2)}, u32[]{:S(2)}) %collective-permute-start.1) | collective-permute-done | bytes 524320 | tf_op jit(solution)/shard_map/ppermute | solution.py:18
  138.8 2.5 copy.38
  141.2 1.1 fusion.92
  142.4 1.4 fusion.7
  143.8 2.5 copy.31
  146.3 1.1 fusion.93
  147.4 0.4 fusion.3
  147.8 0.6 copy-done.5
  148.6 1.5 fusion.25
  150.1 1.5 copy.70
  152.3 0.6 copy.71
  152.9 2.8 fusion.21
  155.7 1.5 copy.63
  157.3 0.6 copy.62
  158.1 0.6 copy.64
  158.8 2.9 %fusion.17 = f32[8,8,256]{0,1,2:T(8,128)} fusion(bf16[2,64,8,256]{1,2,0,3:T(8,128)(2,1)S(1)} %multiply_convert_fusion, bf16[1,64,8,256]{1,2,0,3:T(8,128)(2,1)} %get-tuple-element.17, bf16[1,64,8,256]{1,2,0,3:T(8,128)(2,1)} %get-tuple-element.16), kind=kOutput, calls=%fused_computation.32 | convolution fusion | flops 4472832 | bytes 1114112 | tf_op jit(solution)/shard_map/cwpf,cwqf->pqf/dot_general | solution.py:61
  161.7 1.5 copy.56
  163.9 0.6 copy.57
  164.5 2.8 fusion.13
  167.3 1.5 copy.49
  169.5 0.6 copy.50
  170.1 2.8 fusion.9
  172.9 1.5 copy.42
  175.1 0.6 copy.43
  175.7 1.7 fusion.5
  178.5 0.6 copy.36
  179.1 1.3 dynamic-slice
  180.4 89.6 %all-reduce.10.cloned.1.call-done = (f32[8,8,128]{2,0,1:T(8,128)}, f32[8,8,128]{2,0,1:T(8,128)}, f32[8,8,128]{2,0,1:T(8,128)}, f32[8,8,128]{2,0,1:T(8,128)}, f32...) async-done(((f32[8,8,128]{2,0,1:T(8,128)}, f32[8,8,128]{2,0,1:T(8,128)}, f32[8,8,128]{2,0,1:T(8,128)}, f32[8,8,128]{2,0,1:T(8,128)}, ...) | async-done | bytes 229392
  270.0 1.3 constant_dynamic-update-slice_fusion.6
  271.3 1.3 constant_dynamic-update-slice_fusion.5
  272.7 1.3 constant_dynamic-update-slice_fusion.4
  274.0 1.3 constant_dynamic-update-slice_fusion.3
  275.3 1.3 constant_dynamic-update-slice_fusion.2
  276.6 1.3 constant_dynamic-update-slice_fusion.1
  278.0 1.3 constant_dynamic-update-slice_fusion
  279.3 0.6 copy-done.8
  (45 shorter events, 6.5 us)
Async XLA Ops:
  6.5 263.5 %all-reduce.10.cloned.1.call-start = ((), (), s32[]{:S(2)}) async-start(), calls=%async_computation | async-start | bytes 458752
  9.2 0.7 copy-start.7
  12.2 53.0 %collective-permute-start.5 = (bf16[2,64,8,256]{3,2,1,0:T(8,128)(2,1)}, bf16[2,64,8,256]{3,2,1,0:T(8,128)(2,1)}, u32[]{:S(2)}, u32[]{:S(2)}) collective-permute-start(bf16[2,64,8,256]{3,2,1,0:T(8,128)(2,1)} %copy.30), channel_id=1, source_target_pairs={{0,464},{8,472},{16,480},{24,488},{32,496},{40,504},{48,0},{56,8},... | collective-permute-start | bytes 1572872 | tf_op jit(solution)/shard_map/ppermute | solution.py:18
  26.0 67.8 %collective-permute-start.4 = (bf16[2,64,8,256]{3,2,1,0:T(8,128)(2,1)}, bf16[2,64,8,256]{3,2,1,0:T(8,128)(2,1)}, u32[]{:S(2)}, u32[]{:S(2)}) collective-permute-start(bf16[2,64,8,256]{3,2,1,0:T(8,128)(2,1)} %copy.30), channel_id=1, source_target_pairs={{0,472},{8,480},{16,488},{24,496},{32,504},{40,0},{48,8},{56,16},{... | collective-permute-start | bytes 1572872 | tf_op jit(solution)/shard_map/ppermute | solution.py:18
  31.1 79.5 %collective-permute-start.3 = (bf16[2,64,8,256]{3,2,1,0:T(8,128)(2,1)}, bf16[2,64,8,256]{3,2,1,0:T(8,128)(2,1)}, u32[]{:S(2)}, u32[]{:S(2)}) collective-permute-start(bf16[2,64,8,256]{3,2,1,0:T(8,128)(2,1)} %copy.30), channel_id=1, source_target_pairs={{0,480},{8,488},{16,496},{24,504},{32,0},{40,8},{48,16},{56,24},{6... | collective-permute-start | bytes 1572872 | tf_op jit(solution)/shard_map/ppermute | solution.py:18
  34.2 93.3 %collective-permute-start.2 = (bf16[2,64,8,256]{3,2,1,0:T(8,128)(2,1)}, bf16[2,64,8,256]{3,2,1,0:T(8,128)(2,1)}, u32[]{:S(2)}, u32[]{:S(2)}) collective-permute-start(bf16[2,64,8,256]{3,2,1,0:T(8,128)(2,1)} %copy.30), channel_id=1, source_target_pairs={{0,488},{8,496},{16,504},{24,0},{32,8},{40,16},{48,24},{56,32},{64... | collective-permute-start | bytes 1572872 | tf_op jit(solution)/shard_map/ppermute | solution.py:18
  36.1 102.6 %collective-permute-start.1 = (bf16[2,64,8,256]{3,2,1,0:T(8,128)(2,1)}, bf16[2,64,8,256]{3,2,1,0:T(8,128)(2,1)}, u32[]{:S(2)}, u32[]{:S(2)}) collective-permute-start(bf16[2,64,8,256]{3,2,1,0:T(8,128)(2,1)} %copy.30), channel_id=1, source_target_pairs={{0,496},{8,504},{16,0},{24,8},{32,16},{40,24},{48,32},{56,40},{64,... | collective-permute-start | bytes 1572872 | tf_op jit(solution)/shard_map/ppermute | solution.py:18
  65.1 78.7 %collective-permute-start = (bf16[2,64,8,256]{3,2,1,0:T(8,128)(2,1)}, bf16[2,64,8,256]{3,2,1,0:T(8,128)(2,1)}, u32[]{:S(2)}, u32[]{:S(2)}) collective-permute-start(bf16[2,64,8,256]{3,2,1,0:T(8,128)(2,1)} %copy.30), channel_id=1, source_target_pairs={{0,504},{8,0},{16,8},{24,16},{32,24},{40,32},{48,40},{56,48},{64,5... | collective-permute-start | bytes 1572872 | tf_op jit(solution)/shard_map/ppermute | solution.py:18
  147.4 1.0 copy-start.5
  147.4 1.2 copy-start.6
  148.6 3.0 %copy-start.4 = (f32[8,8,256]{0,1,2:T(8,128)S(1)}, f32[8,8,256]{0,1,2:T(8,128)}, u32[]{:S(2)}) copy-start(f32[8,8,256]{0,1,2:T(8,128)} %fusion.23) | copy-start | bytes 196612
  152.9 4.3 %copy-start.3 = (f32[8,8,256]{0,1,2:T(8,128)S(1)}, f32[8,8,256]{0,1,2:T(8,128)}, u32[]{:S(2)}) copy-start(f32[8,8,256]{0,1,2:T(8,128)} %fusion.19) | copy-start | bytes 196612
  158.8 4.4 %copy-start.2 = (f32[8,8,256]{0,1,2:T(8,128)S(1)}, f32[8,8,256]{0,1,2:T(8,128)}, u32[]{:S(2)}) copy-start(f32[8,8,256]{0,1,2:T(8,128)} %fusion.15) | copy-start | bytes 196612
  164.5 4.3 %copy-start.1 = (f32[8,8,256]{0,1,2:T(8,128)S(1)}, f32[8,8,256]{0,1,2:T(8,128)}, u32[]{:S(2)}) copy-start(f32[8,8,256]{0,1,2:T(8,128)} %fusion.11) | copy-start | bytes 196612
  170.1 4.4 %copy-start = (f32[8,8,256]{0,1,2:T(8,128)S(1)}, f32[8,8,256]{0,1,2:T(8,128)}, u32[]{:S(2)}) copy-start(f32[8,8,256]{0,1,2:T(8,128)} %fusion.7) | copy-start | bytes 196612
  279.3 0.6 copy-start.8
Sparse Core Ops, SparseCore 0:
  179.2 90.7 all-reduce.9
where the time goes:
time: 292 us; the launch traced here: 287 us
  waiting for transfers between devices  161 us (55%)
  local copies, waits for them, and re-layouts  46.9 us (16%)
  starting transfers between devices  31.8 us (11%)
  matrix products  25 us (9%)
  between operations  13.7 us (5%)
  other arithmetic  8.53 us (3%)
    unnamed x2, waiting for transfers between devices  89.6 us
    ppermute x6, waiting for transfers between devices, passed_along(): return lax.ppermute(value, axis, pairs)  71.1 us
    ppermute x6, starting transfers between devices, passed_along(): return lax.ppermute(value, axis, pairs)  31.8 us
    dot_general x7, matrix products, body(): jnp.einsum('cwpf,cwqf->pqf', whitened, flipped, preferred_element_type=jn...  15.1 us
    ppermute x6, local copies, waits for them, and re-layouts, passed_along(): return lax.ppermute(value, axis, pairs)  14.9 us
    unnamed x26, local copies, waits for them, and re-layouts  13.3 us
    mul x6, local copies, waits for them, and re-layouts, body(): imag_part = imag_part * win_scale  8 us
    dot_general x7, matrix products, body(): jnp.einsum('cwpf,cwqf->pqf', whitened, partner, preferred_element_type=jn...  7.98 us
  transfers between devices with their start and end apart: 7, of which 6 were waited for; matrix products, arithmetic and copies ran while one was open for 10% of the time, Pallas kernels for 0%

commit v1 on v0

v1 whole, which is shorter than its diff:
```python
import math

import jax
import jax.numpy as jnp
from jax import lax
from jax.experimental import pallas as pl
from jax.experimental.pallas import tpu as pltpu
from jax.sharding import PartitionSpec as P

WIN = 64
ROUNDS = 6
BAND_BINS = 128
LAGS = 128
NBINS = 2048
S_DEV = 8
LINES = 2 * WIN
GROUP = 8
GROUPS = BAND_BINS // GROUP
PIECE = S_DEV * GROUP
ROWS = 2 * PIECE
VMEM_LIMIT = 48 * 1024 * 1024


def core_index():
    return lax.rem(lax.axis_index("pair"), 2)


def whiten_kernel(spectra_ref, valid_ref, same_ref, cross_ref, lines_ref):
    core = core_index()
    values = spectra_ref[...].astype(jnp.float32)
    magnitude = jnp.sqrt(values[0] * values[0] + values[1] * values[1])
    for half in range(2):
        cut = slice(half * BAND_BINS, (half + 1) * BAND_BINS)
        band_mean = jnp.sum(magnitude[:, :, cut], axis=-1, keepdims=True) * (1.0 / BAND_BINS)
        factor = 1.0 / (band_mean + 1e-06)
        scaled = values[:, :, :, cut] * factor[None]
        lines_ref[half] = scaled.reshape(LINES * S_DEV, BAND_BINS)
    usable = valid_ref[...].astype(jnp.float32)
    usable = jnp.concatenate([usable, usable], axis=1)
    for out_ref, half in ((same_ref, core), (cross_ref, 1 - core)):
        for pair in range(S_DEV // 2):
            parts = []
            for station in (2 * pair, 2 * pair + 1):
                lines = lines_ref[half, pl.ds(station, LINES, stride=S_DEV), :]
                turned = lines.T * usable[station : station + 1, :]
                parts.append(turned.reshape(GROUPS, GROUP, LINES))
            both = jnp.concatenate(parts, axis=1).astype(jnp.bfloat16)
            out_ref[:, pair * 2 * GROUP : (pair + 1) * 2 * GROUP, :] = both


def whiten(spectra, valid):
    piece = jax.ShapeDtypeStruct((GROUPS, PIECE, LINES), jnp.bfloat16)
    return pl.pallas_call(
        whiten_kernel,
        out_shape=(piece, piece),
        in_specs=[pl.BlockSpec(memory_space=pltpu.VMEM)] * 2,
        out_specs=[pl.BlockSpec(memory_space=pltpu.VMEM)] * 2,
        scratch_shapes=[pltpu.VMEM((2, LINES * S_DEV, BAND_BINS), jnp.float32)],
        compiler_params=pltpu.CompilerParams(vmem_limit_bytes=VMEM_LIMIT),
    )(spectra, valid)


def cross_kernel(late, *refs):
    count = 3 if late else 2
    piece_refs = refs[: 2 * count]
    table_ref, out_ref, held, left, turned, sems = refs[2 * count :]
    core = core_index()
    copies = []
    for index in range(count):
        for which in range(2):
            parity = core if which == 0 else 1 - core
            start = pl.multiple_of(parity * PIECE, PIECE)
            copy = pltpu.make_async_copy(
                piece_refs[2 * index + which],
                held.at[index, :, pl.ds(start, PIECE), :],
                sems.at[2 * index + which],
            )
            copy.start()
            copies.append(copy)
    for copy in copies:
        copy.wait()
    if late:
        pairs = ((2 * core, 2 - 2 * core), (1 + core, 2 - core))
    else:
        pairs = ((0, 0), (1 - core, core))

    row = lax.broadcasted_iota(jnp.int32, (ROWS, ROWS), 0)
    col = lax.broadcasted_iota(jnp.int32, (ROWS, ROWS), 1)
    swap_rows = (col == (row % 16) * GROUP + row // 16).astype(jnp.bfloat16)
    lane = lax.broadcasted_iota(jnp.int32, (16, ROWS), 1)
    sign = jnp.where(lax.broadcasted_iota(jnp.int32, (ROWS, LINES), 1) < WIN, -1.0, 1.0)

    for number, (p_side, q_side) in enumerate(pairs):
        for group in range(GROUPS):
            plain = jnp.dot(
                swap_rows, held[p_side, group], preferred_element_type=jnp.float32
            )
            flipped = pltpu.roll(plain, WIN, 1) * sign
            left[number, group, :ROWS, :] = plain.astype(jnp.bfloat16)
            left[number, group, ROWS:, :] = flipped.astype(jnp.bfloat16)

    for group in range(GROUPS):
        picked = []
        for number, (p_side, q_side) in enumerate(pairs):
            full = lax.dot_general(
                left[number, group],
                held[q_side, group],
                (((1,), (1,)), ((), ())),
                preferred_element_type=jnp.float32,
            )
            for part in range(2):
                total = jnp.zeros((16, ROWS), jnp.float32)
                for line in range(GROUP):
                    first = part * ROWS + line * 16
                    total = jnp.where(
                        lane % GROUP == line, full[first : first + 16, :], total
                    )
                picked.append(total)
        stacked = jnp.concatenate([picked[0], picked[2], picked[1], picked[3]], axis=0)
        turned[:, group * GROUP : (group + 1) * GROUP, :] = stacked.T.reshape(16, GROUP, 64)

    table = table_ref[...]
    for q in range(16):
        lines = turned[q].T
        lagged = jnp.dot(
            lines, table, precision=lax.Precision.HIGHEST, preferred_element_type=jnp.float32
        )
        summed = lagged[:32, :LAGS] + lagged[32:, LAGS:]
        for number in range(2):
            for parity in range(2):
                first = number * 16 + parity * 8
                out_ref[parity * 8 + q % 8, number * 2 + q // 8] = summed[first : first + 8, :]


def cross(late, pieces, table):
    count = len(pieces) // 2
    return pl.pallas_call(
        lambda *refs: cross_kernel(late, *refs),
        out_shape=jax.ShapeDtypeStruct((16, 4, S_DEV, LAGS), jnp.float32),
        in_specs=[pl.BlockSpec(memory_space=pl.ANY)] * (2 * count)
        + [pl.BlockSpec(memory_space=pltpu.VMEM)],
        out_specs=pl.BlockSpec(memory_space=pltpu.VMEM),
        scratch_shapes=[
            pltpu.VMEM((count, GROUPS, ROWS, LINES), jnp.bfloat16),
            pltpu.VMEM((2, GROUPS, 2 * ROWS, LINES), jnp.bfloat16),
            pltpu.VMEM((16, BAND_BINS, 64), jnp.float32),
            pltpu.SemaphoreType.DMA((2 * count,)),
        ],
        compiler_params=pltpu.CompilerParams(vmem_limit_bytes=VMEM_LIMIT),
        cost_estimate=pl.CostEstimate(
            flops=2 * 2 * GROUPS * 3 * ROWS * ROWS * LINES,
            bytes_accessed=count * 524288 + 262144,
            transcendentals=0,
        ),
    )(*pieces, table)


def gather_kernel(early_ref, late_ref, home_ref, one_ref, two_ref):
    def summed(ref, half):
        total = ref[half * 8]
        for index in range(1, 8):
            total = total + ref[half * 8 + index]
        return total

    early = [summed(early_ref, half) for half in range(2)]
    late = [summed(late_ref, half) for half in range(2)]
    home_ref[0:2] = early[0][0:2] + early[1][0:2]
    home_ref[2:4] = early[1][2:4]
    home_ref[4:6] = late[0][0:2]
    one_ref[0:2] = early[0][2:4]
    one_ref[2:4] = late[0][2:4]
    two_ref[...] = late[1]


def gather(early, late):
    def shape(count):
        return jax.ShapeDtypeStruct((count, S_DEV, LAGS), jnp.float32)

    return pl.pallas_call(
        gather_kernel,
        out_shape=(shape(6), shape(4), shape(4)),
        compiler_params=pltpu.CompilerParams(vmem_limit_bytes=VMEM_LIMIT),
    )(early, late)


def finish_kernel(home_ref, one_ref, two_ref, out_ref, slots):
    core = core_index()
    band = lax.axis_index("band")
    scale = 1.0 / (math.sqrt(WIN) * math.sqrt(NBINS))
    slots[0:2] = home_ref[0:2]
    slots[2:4] = home_ref[2:4] + one_ref[0:2]
    slots[4:6] = home_ref[4:6] + two_ref[0:2]
    slots[6:8] = one_ref[2:4] + two_ref[2:4]
    for round_no in range(ROUNDS + 1):
        value = slots[round_no + core] * scale
        if round_no == 0:
            row = lax.broadcasted_iota(jnp.int32, (S_DEV, LAGS), 0)
            value = jnp.where(row == band, 0.0, value)
        out_ref[round_no] = value


def finish(home, one, two):
    return pl.pallas_call(
        finish_kernel,
        out_shape=jax.ShapeDtypeStruct((ROUNDS + 1, S_DEV, LAGS), jnp.float32),
        scratch_shapes=[pltpu.VMEM((8, S_DEV, LAGS), jnp.float32)],
        compiler_params=pltpu.CompilerParams(vmem_limit_bytes=VMEM_LIMIT),
    )(home, one, two)


def send(value, steps, other=False):
    count = lax.axis_size("pair")
    pairs = []
    for source in range(count):
        core = source % 2
        target = source - core + 2 * steps[core] + (1 - core if other else core)
        pairs.append((source, target % count))
    return lax.ppermute(value, "pair", pairs)


def exchange(value):
    bands = lax.axis_size("band")
    groups = [
        [(2 * chip + core) * bands + band for core in range(2) for band in range(bands)]
        for chip in range(lax.axis_size("pair") // 2)
    ]
    return lax.all_to_all(
        value, ("pair", "band"), 0, 0, tiled=True, axis_index_groups=groups
    )


def lag_table(first_bin):
    freq = first_bin + jnp.arange(BAND_BINS, dtype=jnp.int32)
    offsets = jnp.arange(LAGS, dtype=jnp.int32) - LAGS // 2
    wrapped = freq[:, None] * offsets[None, :] % (2 * NBINS)
    phase = math.pi * wrapped.astype(jnp.float32) / NBINS
    return jnp.concatenate([jnp.cos(phase), -jnp.sin(phase)], axis=1)


def body(spectra, validity):
    same, other = whiten(spectra, validity.T)
    core = core_index()
    first_bin = (lax.axis_index("band") * 2 + core) * BAND_BINS
    table = lag_table(first_bin)
    near_same = send(same, (1, -1))
    near_other = send(other, (-1, 1), other=True)
    own_other = send(other, (0, 0), other=True)
    far_same = send(same, (-2, 2))
    far_other = send(other, (2, -2), other=True)
    own = [same, own_other]
    near = [near_same, near_other]
    far = [far_same, far_other]
    early = exchange(cross(False, own + near, table))
    late = exchange(cross(True, own + near + far, table))
    home, one, two = gather(early, late)
    one = send(one, (-1, -1))
    two = send(two, (-2, -2))
    return finish(home, one, two).reshape(ROUNDS + 1, S_DEV, 1, LAGS)


def solution(mesh):
    return jax.shard_map(
        body,
        mesh=mesh,
        in_specs=(P(None, None, "pair", "band"), P(None, "pair")),
        out_specs=P(None, "pair", "band", None),
        check_vma=False,
    )
```

time: 292 us -> 77.6 us (0.27)
  the two profiles are of different devices: /device:TPU:1 before, /device:TPU:2 now
where the time goes in v1:
time: 77.6 us; the launch traced here: 77.1 us
  starting transfers between devices  35.3 us (45%)
  waiting for transfers between devices  20.8 us (27%)
  blocking collectives  12.2 us (16%)
  Pallas kernels  6.64 us (9%)
  local copies, waits for them, and re-layouts  1.73 us (2%)
    ppermute x7, starting transfers between devices, send(): return lax.ppermute(value, 'pair', pairs)  28.8 us
    ppermute x7, waiting for transfers between devices, send(): return lax.ppermute(value, 'pair', pairs)  13.7 us
    all_to_all x1, blocking collectives, exchange(): lax.all_to_all(value, ('pair', 'band'), 0, 0, tiled=True, axis_index_grou...  12.2 us
    all_to_all x1, waiting for transfers between devices, exchange(): lax.all_to_all(value, ('pair', 'band'), 0, 0, tiled=True, axis_index_grou...  7.11 us
    all_to_all x1, starting transfers between devices, exchange(): lax.all_to_all(value, ('pair', 'band'), 0, 0, tiled=True, axis_index_grou...  6.44 us
    pallas_call x2, Pallas kernels, cross(): pl.pallas_call(lambda *refs: cross_kernel(late, *refs), out_shape=jax.Sha...  5.33 us
    unnamed x4, local copies, waits for them, and re-layouts  1.73 us
  transfers between devices with their start and end apart: 8, of which 3 were waited for; matrix products, arithmetic and copies ran while one was open for 0% of the time, Pallas kernels for 7%

profile of v1, /device:TPU:2, one launch (start us, length us, event | category | flops | bytes accessed | tf_op | source)
XLA Modules:
  0.0 77.1 jit_solution(13953906760394394434)
XLA Ops:
  0.0 0.0 copy-start
  0.0 1.0 %copy-done = bf16[2,64,8,256]{3,2,1,0:T(8,128)(2,1)S(1)} copy-done((bf16[2,64,8,256]{3,2,1,0:T(8,128)(2,1)S(1)}, bf16[2,64,8,256]{3,2,1,0:T(8,128)(2,1)}, u32[]{:S(2)}) %copy-start) | copy-done | bytes 524312
  1.0 0.0 copy-start.1
  1.0 0.7 copy-done.1
  1.7 0.7 shard_map.28
  2.4 4.6 %collective-permute-start.4 = (bf16[16,64,128]{2,1,0:T(8,128)(2,1)S(1)}, bf16[16,64,128]{2,1,0:T(8,128)(2,1)S(1)}, u32[]{:S(2)}, u32[]{:S(2)}) collective-permute-start(bf16[16,64,128]{2,1,0:T(8,128)(2,1)S(1)} %get-tuple-element.11), channel_id=1, source_target_pairs={{0,40},{8,480},{16,56},{24,496},{32,72},{40,0},{48,88},{56,16},{64... | collective-permute-start | bytes 786440 | tf_op jit(solution)/shard_map/ppermute | solution.py:218
  7.0 9.8 %collective-permute-start.2 = (bf16[16,64,128]{2,1,0:T(8,128)(2,1)S(1)}, bf16[16,64,128]{2,1,0:T(8,128)(2,1)S(1)}, u32[]{:S(2)}, u32[]{:S(2)}) collective-permute-start(bf16[16,64,128]{2,1,0:T(8,128)(2,1)S(1)} %get-tuple-element.11), channel_id=1, source_target_pairs={{0,504},{8,16},{16,8},{24,32},{32,24},{40,48},{48,40},{56,64},{64,... | collective-permute-start | bytes 786440 | tf_op jit(solution)/shard_map/ppermute | solution.py:218
  16.9 1.9 %collective-permute-start = (bf16[16,64,128]{2,1,0:T(8,128)(2,1)S(1)}, bf16[16,64,128]{2,1,0:T(8,128)(2,1)S(1)}, u32[]{:S(2)}, u32[]{:S(2)}) collective-permute-start(bf16[16,64,128]{2,1,0:T(8,128)(2,1)S(1)} %get-tuple-element.11), channel_id=1, source_target_pairs={{0,8},{8,0},{16,24},{24,16},{32,40},{40,32},{48,56},{56,48},{64,72... | collective-permute-start | bytes 786440 | tf_op jit(solution)/shard_map/ppermute | solution.py:218
  18.8 4.6 %collective-permute-start.3 = (bf16[16,64,128]{2,1,0:T(8,128)(2,1)S(1)}, bf16[16,64,128]{2,1,0:T(8,128)(2,1)S(1)}, u32[]{:S(2)}, u32[]{:S(2)}) collective-permute-start(bf16[16,64,128]{2,1,0:T(8,128)(2,1)S(1)} %get-tuple-element.10.refs_0_), channel_id=1, source_target_pairs={{0,480},{8,40},{16,496},{24,56},{32,0},{40,72},{48,16},{56,88},{64... | collective-permute-start | bytes 786440 | tf_op jit(solution)/shard_map/ppermute | solution.py:218
  23.4 1.9 %collective-permute-start.1 = (bf16[16,64,128]{2,1,0:T(8,128)(2,1)S(1)}, bf16[16,64,128]{2,1,0:T(8,128)(2,1)S(1)}, u32[]{:S(2)}, u32[]{:S(2)}) collective-permute-start(bf16[16,64,128]{2,1,0:T(8,128)(2,1)S(1)} %get-tuple-element.10.refs_0_), channel_id=1, source_target_pairs={{0,16},{8,504},{16,32},{24,8},{32,48},{40,24},{48,64},{56,40},{64,... | collective-permute-start | bytes 786440 | tf_op jit(solution)/shard_map/ppermute | solution.py:218
  25.3 0.3 fusion.3
  25.7 0.0 collective-permute-done.2.refs_3_
  25.7 0.0 collective-permute-done.refs_1_
  25.7 9.1 %collective-permute-done.1.refs_2_ = bf16[16,64,128]{2,1,0:T(8,128)(2,1)S(1)} collective-permute-done((bf16[16,64,128]{2,1,0:T(8,128)(2,1)S(1)}, bf16[16,64,128]{2,1,0:T(8,128)(2,1)S(1)}, u32[]{:S(2)}, u32[]{:S(2)}) %collective-permute-start.1) | collective-permute-done | bytes 262176 | tf_op jit(solution)/shard_map/ppermute | solution.py:218
  34.8 3.0 %shard_map.29 = f32[16,4,8,128]{3,2,1,0:T(8,128)} custom-call(bf16[16,64,128]{2,1,0:T(8,128)(2,1)S(1)} %get-tuple-element.10.refs_0_, bf16[16,64,128]{2,1,0:T(8,128)(2,1)S(1)} %collective-permute-done.refs_1_, bf16[16,64,128]{2,1,0:T(8,128)(2,1)S(1)} %collective-permute-done.1.refs_2_, bf16[16,64,128]{2,1,0:T(8,128)(2,1)S(1)} %collective-permute-done.2.refs_3_, ...), custom_call_target="tpu_custom_call" | custom-call | flops 402653184 | bytes 1310720 | tf_op jit(solution)/shard_map/pallas_call | solution.py:137
  37.8 6.4 %all-to-all-start = ((f32[16,4,8,128]{3,2,1,0:T(8,128)}), f32[16,4,8,128]{3,2,1,0:T(8,128)S(1)}, u32[]{:S(2)}, u32[]{:S(2)}) async-start(f32[16,4,8,128]{3,2,1,0:T(8,128)} %shard_map.29), calls=%async_computation | async-start | bytes 524288 | tf_op jit(solution)/shard_map/all_to_all | solution.py:227
  44.2 0.0 collective-permute-done.4.refs_5_
  44.2 0.0 collective-permute-done.3.refs_4_
  44.2 2.4 %shard_map.30 = f32[16,4,8,128]{3,2,1,0:T(8,128)S(1)} custom-call(bf16[16,64,128]{2,1,0:T(8,128)(2,1)S(1)} %get-tuple-element.10.refs_0_, bf16[16,64,128]{2,1,0:T(8,128)(2,1)S(1)} %collective-permute-done.refs_1_, bf16[16,64,128]{2,1,0:T(8,128)(2,1)S(1)} %collective-permute-done.1.refs_2_, bf16[16,64,128]{2,1,0:T(8,128)(2,1)S(1)} %collective-permute-done.2.refs_3_, ...), custom_call_target="tpu_custom_call" | custom-call | flops 402653184 | bytes 1835008 | tf_op jit(solution)/shard_map/pallas_call | solution.py:137
  46.6 7.1 %all-to-all-done.early_ref = f32[16,4,8,128]{3,2,1,0:T(8,128)S(1)} async-done(((f32[16,4,8,128]{3,2,1,0:T(8,128)}), f32[16,4,8,128]{3,2,1,0:T(8,128)S(1)}, u32[]{:S(2)}, u32[]{:S(2)}) %all-to-all-start) | async-done | bytes 262176 | tf_op jit(solution)/shard_map/all_to_all | solution.py:227
  53.7 12.2 %all_to_all.10.late_ref = f32[16,4,8,128]{3,2,1,0:T(8,128)S(1)} all-to-all(f32[16,4,8,128]{3,2,1,0:T(8,128)S(1)} %shard_map.30), channel_id=1, replica_groups={{0,1,2,3,4,5,6,7,8,9,10,11,12,13,14,15},{16,17,18,19,20,21,22,23,24,25,..., dimensions={0} | all-to-all | bytes 524288 | tf_op jit(solution)/shard_map/all_to_all | solution.py:227
  65.9 4.1 %collective-permute-start.5 = (f32[4,8,128]{2,1,0:T(8,128)S(1)}, f32[4,8,128]{2,1,0:T(8,128)S(1)}, u32[]{:S(2)}, u32[]{:S(2)}) collective-permute-start(f32[4,8,128]{2,1,0:T(8,128)S(1)} %get-tuple-element.13), channel_id=1, source_target_pairs={{0,496},{8,504},{16,0},{24,8},{32,16},{40,24},{48,32},{56,40},{64,... | collective-permute-start | bytes 49160 | tf_op jit(solution)/shard_map/ppermute | solution.py:218
  70.0 1.9 %collective-permute-start.6 = (f32[4,8,128]{2,1,0:T(8,128)S(1)}, f32[4,8,128]{2,1,0:T(8,128)S(1)}, u32[]{:S(2)}, u32[]{:S(2)}) collective-permute-start(f32[4,8,128]{2,1,0:T(8,128)S(1)} %get-tuple-element.14), channel_id=1, source_target_pairs={{0,480},{8,488},{16,496},{24,504},{32,0},{40,8},{48,16},{56,24},{6... | collective-permute-start | bytes 49160 | tf_op jit(solution)/shard_map/ppermute | solution.py:218
  71.9 0.0 collective-permute-done.5.one_ref
  71.9 4.6 %collective-permute-done.6.two_ref = f32[4,8,128]{2,1,0:T(8,128)S(1)} collective-permute-done((f32[4,8,128]{2,1,0:T(8,128)S(1)}, f32[4,8,128]{2,1,0:T(8,128)S(1)}, u32[]{:S(2)}, u32[]{:S(2)}) %collective-permute-start.6) | collective-permute-done | bytes 16416 | tf_op jit(solution)/shard_map/ppermute | solution.py:218
  76.5 0.6 shard_map.32
  (3 shorter events, 0.0 us)
Async XLA Ops:
  0.0 1.0 %copy-start = (bf16[2,64,8,256]{3,2,1,0:T(8,128)(2,1)S(1)}, bf16[2,64,8,256]{3,2,1,0:T(8,128)(2,1)}, u32[]{:S(2)}) copy-start(bf16[2,64,8,256]{3,2,1,0:T(8,128)(2,1)} %spectra_ref.1) | copy-start | bytes 1572868
  1.0 0.7 copy-start.1
  2.4 41.8 %collective-permute-start.4 = (bf16[16,64,128]{2,1,0:T(8,128)(2,1)S(1)}, bf16[16,64,128]{2,1,0:T(8,128)(2,1)S(1)}, u32[]{:S(2)}, u32[]{:S(2)}) collective-permute-start(bf16[16,64,128]{2,1,0:T(8,128)(2,1)S(1)} %get-tuple-element.11), channel_id=1, source_target_pairs={{0,40},{8,480},{16,56},{24,496},{32,72},{40,0},{48,88},{56,16},{64... | collective-permute-start | bytes 786440 | tf_op jit(solution)/shard_map/ppermute | solution.py:218
  7.0 18.7 %collective-permute-start.2 = (bf16[16,64,128]{2,1,0:T(8,128)(2,1)S(1)}, bf16[16,64,128]{2,1,0:T(8,128)(2,1)S(1)}, u32[]{:S(2)}, u32[]{:S(2)}) collective-permute-start(bf16[16,64,128]{2,1,0:T(8,128)(2,1)S(1)} %get-tuple-element.11), channel_id=1, source_target_pairs={{0,504},{8,16},{16,8},{24,32},{32,24},{40,48},{48,40},{56,64},{64,... | collective-permute-start | bytes 786440 | tf_op jit(solution)/shard_map/ppermute | solution.py:218
  16.9 8.8 %collective-permute-start = (bf16[16,64,128]{2,1,0:T(8,128)(2,1)S(1)}, bf16[16,64,128]{2,1,0:T(8,128)(2,1)S(1)}, u32[]{:S(2)}, u32[]{:S(2)}) collective-permute-start(bf16[16,64,128]{2,1,0:T(8,128)(2,1)S(1)} %get-tuple-element.11), channel_id=1, source_target_pairs={{0,8},{8,0},{16,24},{24,16},{32,40},{40,32},{48,56},{56,48},{64,72... | collective-permute-start | bytes 786440 | tf_op jit(solution)/shard_map/ppermute | solution.py:218
  18.8 25.4 %collective-permute-start.3 = (bf16[16,64,128]{2,1,0:T(8,128)(2,1)S(1)}, bf16[16,64,128]{2,1,0:T(8,128)(2,1)S(1)}, u32[]{:S(2)}, u32[]{:S(2)}) collective-permute-start(bf16[16,64,128]{2,1,0:T(8,128)(2,1)S(1)} %get-tuple-element.10.refs_0_), channel_id=1, source_target_pairs={{0,480},{8,40},{16,496},{24,56},{32,0},{40,72},{48,16},{56,88},{64... | collective-permute-start | bytes 786440 | tf_op jit(solution)/shard_map/ppermute | solution.py:218
  23.4 11.4 %collective-permute-start.1 = (bf16[16,64,128]{2,1,0:T(8,128)(2,1)S(1)}, bf16[16,64,128]{2,1,0:T(8,128)(2,1)S(1)}, u32[]{:S(2)}, u32[]{:S(2)}) collective-permute-start(bf16[16,64,128]{2,1,0:T(8,128)(2,1)S(1)} %get-tuple-element.10.refs_0_), channel_id=1, source_target_pairs={{0,16},{8,504},{16,32},{24,8},{32,48},{40,24},{48,64},{56,40},{64,... | collective-permute-start | bytes 786440 | tf_op jit(solution)/shard_map/ppermute | solution.py:218
  37.8 15.9 %all-to-all-start = ((f32[16,4,8,128]{3,2,1,0:T(8,128)}), f32[16,4,8,128]{3,2,1,0:T(8,128)S(1)}, u32[]{:S(2)}, u32[]{:S(2)}) async-start(f32[16,4,8,128]{3,2,1,0:T(8,128)} %shard_map.29), calls=%async_computation | async-start | bytes 524288 | tf_op jit(solution)/shard_map/all_to_all | solution.py:227
  65.9 6.0 %collective-permute-start.5 = (f32[4,8,128]{2,1,0:T(8,128)S(1)}, f32[4,8,128]{2,1,0:T(8,128)S(1)}, u32[]{:S(2)}, u32[]{:S(2)}) collective-permute-start(f32[4,8,128]{2,1,0:T(8,128)S(1)} %get-tuple-element.13), channel_id=1, source_target_pairs={{0,496},{8,504},{16,0},{24,8},{32,16},{40,24},{48,32},{56,40},{64,... | collective-permute-start | bytes 49160 | tf_op jit(solution)/shard_map/ppermute | solution.py:218
  70.0 6.5 %collective-permute-start.6 = (f32[4,8,128]{2,1,0:T(8,128)S(1)}, f32[4,8,128]{2,1,0:T(8,128)S(1)}, u32[]{:S(2)}, u32[]{:S(2)}) collective-permute-start(f32[4,8,128]{2,1,0:T(8,128)S(1)} %get-tuple-element.14), channel_id=1, source_target_pairs={{0,480},{8,488},{16,496},{24,504},{32,0},{40,8},{48,16},{56,24},{6... | collective-permute-start | bytes 49160 | tf_op jit(solution)/shard_map/ppermute | solution.py:218

commit v2 on v1

--- a/solution.py
+++ b/solution.py
@@ -18,6 +18,8 @@
 GROUPS = BAND_BINS // GROUP
 PIECE = S_DEV * GROUP
 ROWS = 2 * PIECE
+CHUNKS = 4
+WHITEN_LIMIT = 52 * 1024 * 1024
 VMEM_LIMIT = 48 * 1024 * 1024
 
 
@@ -25,19 +27,37 @@
     return lax.rem(lax.axis_index("pair"), 2)
 
 
-def whiten_kernel(spectra_ref, valid_ref, same_ref, cross_ref, lines_ref):
+def whiten_kernel(spectra_hbm, valid_hbm, *refs):
+    out_refs, (raw, valid, lines_ref, sems) = refs[:6], refs[6:]
     core = core_index()
-    values = spectra_ref[...].astype(jnp.float32)
-    magnitude = jnp.sqrt(values[0] * values[0] + values[1] * values[1])
-    for half in range(2):
-        cut = slice(half * BAND_BINS, (half + 1) * BAND_BINS)
-        band_mean = jnp.sum(magnitude[:, :, cut], axis=-1, keepdims=True) * (1.0 / BAND_BINS)
-        factor = 1.0 / (band_mean + 1e-06)
-        scaled = values[:, :, :, cut] * factor[None]
-        lines_ref[half] = scaled.reshape(LINES * S_DEV, BAND_BINS)
-    usable = valid_ref[...].astype(jnp.float32)
+    step = WIN // CHUNKS
+    copies = []
+    for chunk in range(CHUNKS):
+        span = pl.ds(chunk * step, step)
+        copies.append(
+            pltpu.make_async_copy(spectra_hbm.at[:, span], raw.at[:, span], sems.at[chunk])
+        )
+        copies[-1].start()
+    copies.append(pltpu.make_async_copy(valid_hbm, valid, sems.at[CHUNKS]))
+    copies[-1].start()
+    for chunk in range(CHUNKS):
+        copies[chunk].wait()
+        values = raw[:, chunk * step : (chunk + 1) * step].astype(jnp.float32)
+        magnitude = jnp.sqrt(values[0] * values[0] + values[1] * values[1])
+        for half in range(2):
+            cut = slice(half * BAND_BINS, (half + 1) * BAND_BINS)
+            band_mean = jnp.sum(magnitude[:, :, cut], axis=-1, keepdims=True) * (1.0 / BAND_BINS)
+            factor = 1.0 / (band_mean + 1e-06)
+            scaled = values[:, :, :, cut] * factor[None]
+            for part in range(2):
+                first = (part * WIN + chunk * step) * S_DEV
+                lines_ref[half, first : first + step * S_DEV, :] = scaled[part].reshape(
+                    step * S_DEV, BAND_BINS
+                )
+    copies[CHUNKS].wait()
+    usable = valid[...].astype(jnp.float32)
     usable = jnp.concatenate([usable, usable], axis=1)
-    for out_ref, half in ((same_ref, core), (cross_ref, 1 - core)):
+    for index, half in enumerate((core, 1 - core)):
         for pair in range(S_DEV // 2):
             parts = []
             for station in (2 * pair, 2 * pair + 1):
@@ -45,25 +65,35 @@
                 turned = lines.T * usable[station : station + 1, :]
                 parts.append(turned.reshape(GROUPS, GROUP, LINES))
             both = jnp.concatenate(parts, axis=1).astype(jnp.bfloat16)
-            out_ref[:, pair * 2 * GROUP : (pair + 1) * 2 * GROUP, :] = both
+            for out_ref in out_refs[index::2]:
+                out_ref[:, pair * 2 * GROUP : (pair + 1) * 2 * GROUP, :] = both
 
 
 def whiten(spectra, valid):
     piece = jax.ShapeDtypeStruct((GROUPS, PIECE, LINES), jnp.bfloat16)
     return pl.pallas_call(
         whiten_kernel,
-        out_shape=(piece, piece),
-        in_specs=[pl.BlockSpec(memory_space=pltpu.VMEM)] * 2,
-        out_specs=[pl.BlockSpec(memory_space=pltpu.VMEM)] * 2,
-        scratch_shapes=[pltpu.VMEM((2, LINES * S_DEV, BAND_BINS), jnp.float32)],
-        compiler_params=pltpu.CompilerParams(vmem_limit_bytes=VMEM_LIMIT),
+        out_shape=(piece,) * 6,
+        in_specs=[pl.BlockSpec(memory_space=pl.ANY)] * 2,
+        out_specs=[pl.BlockSpec(memory_space=pltpu.VMEM)] * 6,
+        scratch_shapes=[
+            pltpu.VMEM((2, WIN, S_DEV, 2 * BAND_BINS), jnp.bfloat16),
+            pltpu.VMEM((S_DEV, WIN), jnp.int32),
+            pltpu.VMEM((2, LINES * S_DEV, BAND_BINS), jnp.float32),
+            pltpu.SemaphoreType.DMA((CHUNKS + 1,)),
+        ],
+        compiler_params=pltpu.CompilerParams(vmem_limit_bytes=WHITEN_LIMIT),
     )(spectra, valid)
 
 
 def cross_kernel(late, *refs):
     count = 3 if late else 2
     piece_refs = refs[: 2 * count]
-    table_ref, out_ref, held, left, turned, sems = refs[2 * count :]
+    if late:
+        table_ref, early_ref, out_ref, held, left, turned, sems = refs[2 * count :]
+        out_ref[...] = early_ref[...]
+    else:
+        table_ref, out_ref, held, left, turned, sems = refs[2 * count :]
     core = core_index()
     copies = []
     for index in range(count):
@@ -80,9 +110,9 @@
     for copy in copies:
         copy.wait()
     if late:
-        pairs = ((2 * core, 2 - 2 * core), (1 + core, 2 - core))
+        pairs = ((1, 1 + core, 2 - core), (3, 1 - core, core))
     else:
-        pairs = ((0, 0), (1 - core, core))
+        pairs = ((0, 1, 1), (2, 1 - core, core))
 
     row = lax.broadcasted_iota(jnp.int32, (ROWS, ROWS), 0)
     col = lax.broadcasted_iota(jnp.int32, (ROWS, ROWS), 1)
@@ -90,7 +120,7 @@
     lane = lax.broadcasted_iota(jnp.int32, (16, ROWS), 1)
     sign = jnp.where(lax.broadcasted_iota(jnp.int32, (ROWS, LINES), 1) < WIN, -1.0, 1.0)
 
-    for number, (p_side, q_side) in enumerate(pairs):
+    for number, (_, p_side, q_side) in enumerate(pairs):
         for group in range(GROUPS):
             plain = jnp.dot(
                 swap_rows, held[p_side, group], preferred_element_type=jnp.float32
@@ -101,7 +131,7 @@
 
     for group in range(GROUPS):
         picked = []
-        for number, (p_side, q_side) in enumerate(pairs):
+        for number, (_, p_side, q_side) in enumerate(pairs):
             full = lax.dot_general(
                 left[number, group],
                 held[q_side, group],
@@ -119,26 +149,37 @@
         stacked = jnp.concatenate([picked[0], picked[2], picked[1], picked[3]], axis=0)
         turned[:, group * GROUP : (group + 1) * GROUP, :] = stacked.T.reshape(16, GROUP, 64)
 
-    table = table_ref[...]
-    for q in range(16):
-        lines = turned[q].T
-        lagged = jnp.dot(
-            lines, table, precision=lax.Precision.HIGHEST, preferred_element_type=jnp.float32
+    table_high = table_ref[...].astype(jnp.bfloat16)
+    table_low = (table_ref[...] - table_high.astype(jnp.float32)).astype(jnp.bfloat16)
+    for first_q in range(0, 16, 4):
+        lines = jnp.concatenate([turned[first_q + step].T for step in range(4)], axis=0)
+        high = lines.astype(jnp.bfloat16)
+        low = (lines - high.astype(jnp.float32)).astype(jnp.bfloat16)
+        lagged = (
+            jnp.dot(high, table_high, preferred_element_type=jnp.float32)
+            + jnp.dot(low, table_high, preferred_element_type=jnp.float32)
+            + jnp.dot(high, table_low, preferred_element_type=jnp.float32)
         )
-        summed = lagged[:32, :LAGS] + lagged[32:, LAGS:]
-        for number in range(2):
-            for parity in range(2):
-                first = number * 16 + parity * 8
-                out_ref[parity * 8 + q % 8, number * 2 + q // 8] = summed[first : first + 8, :]
-
-
-def cross(late, pieces, table):
+        for step in range(4):
+            q = first_q + step
+            part = lagged[step * 64 : (step + 1) * 64]
+            summed = part[:32, :LAGS] + part[32:, LAGS:]
+            for number, (apart, _, _) in enumerate(pairs):
+                for parity in range(2):
+                    round_no = 2 * apart + q // 8 - parity
+                    if 0 <= round_no <= ROUNDS:
+                        first = number * 16 + parity * 8
+                        out_ref[parity * 8 + q % 8, round_no] = summed[first : first + 8, :]
+
+
+def cross(pieces, table, early=None):
     count = len(pieces) // 2
+    late = [] if early is None else [early]
     return pl.pallas_call(
-        lambda *refs: cross_kernel(late, *refs),
-        out_shape=jax.ShapeDtypeStruct((16, 4, S_DEV, LAGS), jnp.float32),
+        lambda *refs: cross_kernel(bool(late), *refs),
+        out_shape=jax.ShapeDtypeStruct((16, ROUNDS + 1, S_DEV, LAGS), jnp.float32),
         in_specs=[pl.BlockSpec(memory_space=pl.ANY)] * (2 * count)
-        + [pl.BlockSpec(memory_space=pltpu.VMEM)],
+        + [pl.BlockSpec(memory_space=pltpu.VMEM)] * (1 + len(late)),
         out_specs=pl.BlockSpec(memory_space=pltpu.VMEM),
         scratch_shapes=[
             pltpu.VMEM((count, GROUPS, ROWS, LINES), jnp.bfloat16),
@@ -152,35 +193,35 @@
             bytes_accessed=count * 524288 + 262144,
             transcendentals=0,
         ),
-    )(*pieces, table)
-
-
-def gather_kernel(early_ref, late_ref, home_ref, one_ref, two_ref):
-    def summed(ref, half):
-        total = ref[half * 8]
+    )(*pieces, table, *late)
+
+
+def gather_kernel(parts_ref, home_ref, one_ref, two_ref, slots):
+    core = core_index()
+    for half in range(2):
+        total = parts_ref[half * 8]
         for index in range(1, 8):
-            total = total + ref[half * 8 + index]
-        return total
-
-    early = [summed(early_ref, half) for half in range(2)]
-    late = [summed(late_ref, half) for half in range(2)]
-    home_ref[0:2] = early[0][0:2] + early[1][0:2]
-    home_ref[2:4] = early[1][2:4]
-    home_ref[4:6] = late[0][0:2]
-    one_ref[0:2] = early[0][2:4]
-    one_ref[2:4] = late[0][2:4]
-    two_ref[...] = late[1]
-
-
-def gather(early, late):
+            total = total + parts_ref[half * 8 + index]
+        slots[half, pl.ds(core, ROUNDS + 1)] = total
+        slots[half, 7 - 7 * core] = jnp.zeros((S_DEV, LAGS), jnp.float32)
+    home_ref[0:2] = slots[0, 0:2] + slots[1, 0:2]
+    home_ref[2:4] = slots[1, 2:4]
+    home_ref[4:6] = slots[0, 4:6]
+    one_ref[0:2] = slots[0, 2:4]
+    one_ref[2:4] = slots[0, 6:8]
+    two_ref[...] = slots[1, 4:8]
+
+
+def gather(parts):
     def shape(count):
         return jax.ShapeDtypeStruct((count, S_DEV, LAGS), jnp.float32)
 
     return pl.pallas_call(
         gather_kernel,
         out_shape=(shape(6), shape(4), shape(4)),
+        scratch_shapes=[pltpu.VMEM((2, 8, S_DEV, LAGS), jnp.float32)],
         compiler_params=pltpu.CompilerParams(vmem_limit_bytes=VMEM_LIMIT),
-    )(early, late)
+    )(parts)
 
 
 def finish_kernel(home_ref, one_ref, two_ref, out_ref, slots):
@@ -238,21 +279,15 @@
 
 
 def body(spectra, validity):
-    same, other = whiten(spectra, validity.T)
-    core = core_index()
-    first_bin = (lax.axis_index("band") * 2 + core) * BAND_BINS
+    far_same, far_other, own_same, own_other, near_same, near_other = whiten(spectra, validity.T)
+    first_bin = (lax.axis_index("band") * 2 + core_index()) * BAND_BINS
     table = lag_table(first_bin)
-    near_same = send(same, (1, -1))
-    near_other = send(other, (-1, 1), other=True)
-    own_other = send(other, (0, 0), other=True)
-    far_same = send(same, (-2, 2))
-    far_other = send(other, (2, -2), other=True)
-    own = [same, own_other]
-    near = [near_same, near_other]
-    far = [far_same, far_other]
-    early = exchange(cross(False, own + near, table))
-    late = exchange(cross(True, own + near + far, table))
-    home, one, two = gather(early, late)
+    far = [send(far_same, (-2, 2)), send(far_other, (2, -2), other=True)]
+    own = [own_same, send(own_other, (0, 0), other=True)]
+    near = [send(near_same, (1, -1)), send(near_other, (-1, 1), other=True)]
+    early = cross(far + own, table)
+    late = cross(far + near + own, table, early)
+    home, one, two = gather(exchange(late))
     one = send(one, (-1, -1))
     two = send(two, (-2, -2))
     return finish(home, one, two).reshape(ROUNDS + 1, S_DEV, 1, LAGS)

time: 77.6 us -> 65.9 us (0.85)
  waiting for transfers between devices: 20.8 us -> 7.72 us
  blocking collectives: 12.2 us -> 17.8 us
  starting transfers between devices: 35.3 us -> 32.3 us
  local copies, waits for them, and re-layouts: 1.73 us -> 0.69 us
    all_to_all x1 -> x0, waiting for transfers between devices: 7.11 us -> none  [exchange(): lax.all_to_all(value, ('pair', 'band'), 0, 0, tiled=True, axis_index_grou...]
    all_to_all x1 -> x0, starting transfers between devices: 6.44 us -> none  [exchange(): lax.all_to_all(value, ('pair', 'band'), 0, 0, tiled=True, axis_index_grou...]
    ppermute x7, waiting for transfers between devices: 13.7 us -> 7.72 us  [send(): return lax.ppermute(value, 'pair', pairs)]
    all_to_all x1, blocking collectives: 12.2 us -> 17.8 us  [exchange(): lax.all_to_all(value, ('pair', 'band'), 0, 0, tiled=True, axis_index_grou...]
    ppermute x7, starting transfers between devices: 28.8 us -> 32.3 us  [send(): return lax.ppermute(value, 'pair', pairs)]
    unnamed x4 -> x2, local copies, waits for them, and re-layouts: 1.73 us -> 0.69 us
  transfers between devices with their start and end apart: 8 -> 7, of which waited for: 3 -> 4; matrix products, arithmetic and copies ran while one was open for 0% -> 1% of each run, Pallas kernels for 7% -> 3%
where the time goes in v2:
time: 65.9 us; the launch traced here: 65.5 us
  starting transfers between devices  32.3 us (49%)
  blocking collectives  17.8 us (27%)
  waiting for transfers between devices  7.72 us (12%)
  Pallas kernels  6.55 us (10%)
  local copies, waits for them, and re-layouts  0.69 us (1%)
    ppermute x7, starting transfers between devices, send(): return lax.ppermute(value, 'pair', pairs)  32.3 us
    all_to_all x1, blocking collectives, exchange(): lax.all_to_all(value, ('pair', 'band'), 0, 0, tiled=True, axis_index_grou...  17.8 us
    ppermute x7, waiting for transfers between devices, send(): return lax.ppermute(value, 'pair', pairs)  7.72 us
    pallas_call x2, Pallas kernels, cross(): pl.pallas_call(lambda *refs: cross_kernel(bool(late), *refs), out_shape=j...  4.02 us
    pallas_call x1, Pallas kernels, whiten(): pl.pallas_call(whiten_kernel, out_shape=(piece,) * 6, in_specs=[pl.BlockS...  1.88 us
  transfers between devices with their start and end apart: 7, of which 4 were waited for; matrix products, arithmetic and copies ran while one was open for 1% of the time, Pallas kernels for 3%

profile of v2, /device:TPU:2, one launch (start us, length us, event | category | flops | bytes accessed | tf_op | source)
XLA Modules:
  0.0 65.5 jit_solution(6301870767415536759)
XLA Ops:
  0.0 0.0 copy-start
  0.0 0.7 %copy-done = s32[64,8]{0,1:T(8,128)S(1)} copy-done((s32[64,8]{0,1:T(8,128)S(1)}, s32[64,8]{0,1:T(8,128)}, u32[]{:S(2)}) %copy-start) | copy-done | bytes 2072
  0.7 1.9 %shard_map.28 = (bf16[16,64,128]{2,1,0:T(8,128)(2,1)S(1)}, bf16[16,64,128]{2,1,0:T(8,128)(2,1)S(1)}, bf16[16,64,128]{2,1,0:T(8,128)(2,1)S(1)}, bf16[16,64,128]{2...) custom-call(bf16[2,64,8,256]{3,2,1,0:T(8,128)(2,1)} %spectra_hbm.1, ...), custom_call_target="tpu_custom_call" | custom-call | tf_op jit(solution)/shard_map/pallas_call | solution.py:74
  2.6 11.8 %collective-permute-start = (bf16[16,64,128]{2,1,0:T(8,128)(2,1)S(1)}, bf16[16,64,128]{2,1,0:T(8,128)(2,1)S(1)}, u32[]{:S(2)}, u32[]{:S(2)}) collective-permute-start(bf16[16,64,128]{2,1,0:T(8,128)(2,1)S(1)} %get-tuple-element.14), channel_id=1, source_target_pairs={{0,480},{8,40},{16,496},{24,56},{32,0},{40,72},{48,16},{56,88},{64... | collective-permute-start | bytes 786440 | tf_op jit(solution)/shard_map/ppermute | solution.py:259
  14.4 1.9 %collective-permute-start.1 = (bf16[16,64,128]{2,1,0:T(8,128)(2,1)S(1)}, bf16[16,64,128]{2,1,0:T(8,128)(2,1)S(1)}, u32[]{:S(2)}, u32[]{:S(2)}) collective-permute-start(bf16[16,64,128]{2,1,0:T(8,128)(2,1)S(1)} %get-tuple-element.15), channel_id=1, source_target_pairs={{0,40},{8,480},{16,56},{24,496},{32,72},{40,0},{48,88},{56,16},{64... | collective-permute-start | bytes 786440 | tf_op jit(solution)/shard_map/ppermute | solution.py:259
  16.3 2.9 %collective-permute-start.2 = (bf16[16,64,128]{2,1,0:T(8,128)(2,1)S(1)}, bf16[16,64,128]{2,1,0:T(8,128)(2,1)S(1)}, u32[]{:S(2)}, u32[]{:S(2)}) collective-permute-start(bf16[16,64,128]{2,1,0:T(8,128)(2,1)S(1)} %get-tuple-element.16), channel_id=1, source_target_pairs={{0,16},{8,504},{16,32},{24,8},{32,48},{40,24},{48,64},{56,40},{64,... | collective-permute-start | bytes 786440 | tf_op jit(solution)/shard_map/ppermute | solution.py:259
  19.3 5.0 %collective-permute-start.3 = (bf16[16,64,128]{2,1,0:T(8,128)(2,1)S(1)}, bf16[16,64,128]{2,1,0:T(8,128)(2,1)S(1)}, u32[]{:S(2)}, u32[]{:S(2)}) collective-permute-start(bf16[16,64,128]{2,1,0:T(8,128)(2,1)S(1)} %get-tuple-element.17), channel_id=1, source_target_pairs={{0,504},{8,16},{16,8},{24,32},{32,24},{40,48},{48,40},{56,64},{64,... | collective-permute-start | bytes 786440 | tf_op jit(solution)/shard_map/ppermute | solution.py:259
  24.3 1.9 %collective-permute-start.4 = (bf16[16,64,128]{2,1,0:T(8,128)(2,1)S(1)}, bf16[16,64,128]{2,1,0:T(8,128)(2,1)S(1)}, u32[]{:S(2)}, u32[]{:S(2)}) collective-permute-start(bf16[16,64,128]{2,1,0:T(8,128)(2,1)S(1)} %get-tuple-element.19), channel_id=1, source_target_pairs={{0,8},{8,0},{16,24},{24,16},{32,40},{40,32},{48,56},{56,48},{64,72... | collective-permute-start | bytes 786440 | tf_op jit(solution)/shard_map/ppermute | solution.py:259
  26.2 0.3 fusion.3
  26.6 0.0 collective-permute-done.refs_0_
  26.6 0.0 collective-permute-done.1.refs_1_
  26.6 1.1 %collective-permute-done.4.refs_3_.refs_5_ = bf16[16,64,128]{2,1,0:T(8,128)(2,1)S(1)} collective-permute-done((bf16[16,64,128]{2,1,0:T(8,128)(2,1)S(1)}, bf16[16,64,128]{2,1,0:T(8,128)(2,1)S(1)}, u32[]{:S(2)}, u32[]{:S(2)}) %collective-permute-start.4) | collective-permute-done | bytes 262176 | tf_op jit(solution)/shard_map/ppermute | solution.py:259
  27.7 2.0 %shard_map.29.refs_7_ = f32[16,7,8,128]{3,2,1,0:T(8,128)S(1)} custom-call(bf16[16,64,128]{2,1,0:T(8,128)(2,1)S(1)} %collective-permute-done.refs_0_, bf16[16,64,128]{2,1,0:T(8,128)(2,1)S(1)} %collective-permute-done.1.refs_1_, bf16[16,64,128]{2,1,0:T(8,128)(2,1)S(1)} %get-tuple-element.18.refs_2_.refs_4_, ...), custom_call_target="tpu_custom_call" | custom-call | flops 402653184 | bytes 1310720 | tf_op jit(solution)/shard_map/pallas_call | solution.py:178
  29.7 1.4 %collective-permute-done.2.refs_2_ = bf16[16,64,128]{2,1,0:T(8,128)(2,1)S(1)} collective-permute-done((bf16[16,64,128]{2,1,0:T(8,128)(2,1)S(1)}, bf16[16,64,128]{2,1,0:T(8,128)(2,1)S(1)}, u32[]{:S(2)}, u32[]{:S(2)}) %collective-permute-start.2) | collective-permute-done | bytes 262176 | tf_op jit(solution)/shard_map/ppermute | solution.py:259
  31.0 0.7 %collective-permute-done.3.refs_3_ = bf16[16,64,128]{2,1,0:T(8,128)(2,1)S(1)} collective-permute-done((bf16[16,64,128]{2,1,0:T(8,128)(2,1)S(1)}, bf16[16,64,128]{2,1,0:T(8,128)(2,1)S(1)}, u32[]{:S(2)}, u32[]{:S(2)}) %collective-permute-start.3) | collective-permute-done | bytes 262176 | tf_op jit(solution)/shard_map/ppermute | solution.py:259
  31.7 2.1 %shard_map.30 = f32[16,7,8,128]{3,2,1,0:T(8,128)S(1)} custom-call(bf16[16,64,128]{2,1,0:T(8,128)(2,1)S(1)} %collective-permute-done.refs_0_, bf16[16,64,128]{2,1,0:T(8,128)(2,1)S(1)} %collective-permute-done.1.refs_1_, bf16[16,64,128]{2,1,0:T(8,128)(2,1)S(1)} %collective-permute-done.2.refs_2_, bf16[16,64,128]{2,1,0:T(8,128)(2,1)S(1)} %collective-permute-done.3.refs_3_, ...), custom_call_target="tpu_custom_call" | custom-call | flops 402653184 | bytes 1835008 | tf_op jit(solution)/shard_map/pallas_call | solution.py:178
  33.8 17.8 %all_to_all.5.parts_ref = f32[16,7,8,128]{3,2,1,0:T(8,128)S(1)} all-to-all(f32[16,7,8,128]{3,2,1,0:T(8,128)S(1)} %shard_map.30), channel_id=1, replica_groups={{0,1,2,3,4,5,6,7,8,9,10,11,12,13,14,15},{16,17,18,19,20,21,22,23,24,25,..., dimensions={0} | all-to-all | bytes 917504 | tf_op jit(solution)/shard_map/all_to_all | solution.py:268
  51.6 6.8 %collective-permute-start.5 = (f32[4,8,128]{2,1,0:T(8,128)S(1)}, f32[4,8,128]{2,1,0:T(8,128)S(1)}, u32[]{:S(2)}, u32[]{:S(2)}) collective-permute-start(f32[4,8,128]{2,1,0:T(8,128)S(1)} %get-tuple-element.21), channel_id=1, source_target_pairs={{0,496},{8,504},{16,0},{24,8},{32,16},{40,24},{48,32},{56,40},{64,... | collective-permute-start | bytes 49160 | tf_op jit(solution)/shard_map/ppermute | solution.py:259
  58.4 1.9 %collective-permute-start.6 = (f32[4,8,128]{2,1,0:T(8,128)S(1)}, f32[4,8,128]{2,1,0:T(8,128)S(1)}, u32[]{:S(2)}, u32[]{:S(2)}) collective-permute-start(f32[4,8,128]{2,1,0:T(8,128)S(1)} %get-tuple-element.22), channel_id=1, source_target_pairs={{0,480},{8,488},{16,496},{24,504},{32,0},{40,8},{48,16},{56,24},{6... | collective-permute-start | bytes 49160 | tf_op jit(solution)/shard_map/ppermute | solution.py:259
  60.3 0.0 collective-permute-done.5.one_ref
  60.3 4.6 %collective-permute-done.6.two_ref = f32[4,8,128]{2,1,0:T(8,128)S(1)} collective-permute-done((f32[4,8,128]{2,1,0:T(8,128)S(1)}, f32[4,8,128]{2,1,0:T(8,128)S(1)}, u32[]{:S(2)}, u32[]{:S(2)}) %collective-permute-start.6) | collective-permute-done | bytes 16416 | tf_op jit(solution)/shard_map/ppermute | solution.py:259
  64.9 0.6 shard_map.32
  (3 shorter events, 0.0 us)
Async XLA Ops:
  0.0 0.7 %copy-start = (s32[64,8]{0,1:T(8,128)S(1)}, s32[64,8]{0,1:T(8,128)}, u32[]{:S(2)}) copy-start(s32[64,8]{0,1:T(8,128)} %param.3) | copy-start | bytes 6148
  2.6 24.0 %collective-permute-start = (bf16[16,64,128]{2,1,0:T(8,128)(2,1)S(1)}, bf16[16,64,128]{2,1,0:T(8,128)(2,1)S(1)}, u32[]{:S(2)}, u32[]{:S(2)}) collective-permute-start(bf16[16,64,128]{2,1,0:T(8,128)(2,1)S(1)} %get-tuple-element.14), channel_id=1, source_target_pairs={{0,480},{8,40},{16,496},{24,56},{32,0},{40,72},{48,16},{56,88},{64... | collective-permute-start | bytes 786440 | tf_op jit(solution)/shard_map/ppermute | solution.py:259
  14.4 12.2 %collective-permute-start.1 = (bf16[16,64,128]{2,1,0:T(8,128)(2,1)S(1)}, bf16[16,64,128]{2,1,0:T(8,128)(2,1)S(1)}, u32[]{:S(2)}, u32[]{:S(2)}) collective-permute-start(bf16[16,64,128]{2,1,0:T(8,128)(2,1)S(1)} %get-tuple-element.15), channel_id=1, source_target_pairs={{0,40},{8,480},{16,56},{24,496},{32,72},{40,0},{48,88},{56,16},{64... | collective-permute-start | bytes 786440 | tf_op jit(solution)/shard_map/ppermute | solution.py:259
  16.3 14.7 %collective-permute-start.2 = (bf16[16,64,128]{2,1,0:T(8,128)(2,1)S(1)}, bf16[16,64,128]{2,1,0:T(8,128)(2,1)S(1)}, u32[]{:S(2)}, u32[]{:S(2)}) collective-permute-start(bf16[16,64,128]{2,1,0:T(8,128)(2,1)S(1)} %get-tuple-element.16), channel_id=1, source_target_pairs={{0,16},{8,504},{16,32},{24,8},{32,48},{40,24},{48,64},{56,40},{64,... | collective-permute-start | bytes 786440 | tf_op jit(solution)/shard_map/ppermute | solution.py:259
  19.3 12.4 %collective-permute-start.3 = (bf16[16,64,128]{2,1,0:T(8,128)(2,1)S(1)}, bf16[16,64,128]{2,1,0:T(8,128)(2,1)S(1)}, u32[]{:S(2)}, u32[]{:S(2)}) collective-permute-start(bf16[16,64,128]{2,1,0:T(8,128)(2,1)S(1)} %get-tuple-element.17), channel_id=1, source_target_pairs={{0,504},{8,16},{16,8},{24,32},{32,24},{40,48},{48,40},{56,64},{64,... | collective-permute-start | bytes 786440 | tf_op jit(solution)/shard_map/ppermute | solution.py:259
  24.3 3.4 %collective-permute-start.4 = (bf16[16,64,128]{2,1,0:T(8,128)(2,1)S(1)}, bf16[16,64,128]{2,1,0:T(8,128)(2,1)S(1)}, u32[]{:S(2)}, u32[]{:S(2)}) collective-permute-start(bf16[16,64,128]{2,1,0:T(8,128)(2,1)S(1)} %get-tuple-element.19), channel_id=1, source_target_pairs={{0,8},{8,0},{16,24},{24,16},{32,40},{40,32},{48,56},{56,48},{64,72... | collective-permute-start | bytes 786440 | tf_op jit(solution)/shard_map/ppermute | solution.py:259
  51.6 8.7 %collective-permute-start.5 = (f32[4,8,128]{2,1,0:T(8,128)S(1)}, f32[4,8,128]{2,1,0:T(8,128)S(1)}, u32[]{:S(2)}, u32[]{:S(2)}) collective-permute-start(f32[4,8,128]{2,1,0:T(8,128)S(1)} %get-tuple-element.21), channel_id=1, source_target_pairs={{0,496},{8,504},{16,0},{24,8},{32,16},{40,24},{48,32},{56,40},{64,... | collective-permute-start | bytes 49160 | tf_op jit(solution)/shard_map/ppermute | solution.py:259
  58.4 6.5 %collective-permute-start.6 = (f32[4,8,128]{2,1,0:T(8,128)S(1)}, f32[4,8,128]{2,1,0:T(8,128)S(1)}, u32[]{:S(2)}, u32[]{:S(2)}) collective-permute-start(f32[4,8,128]{2,1,0:T(8,128)S(1)} %get-tuple-element.22), channel_id=1, source_target_pairs={{0,480},{8,488},{16,496},{24,504},{32,0},{40,8},{48,16},{56,24},{6... | collective-permute-start | bytes 49160 | tf_op jit(solution)/shard_map/ppermute | solution.py:259

commit v3 on v2

--- a/solution.py
+++ b/solution.py
@@ -86,33 +86,30 @@
     )(spectra, valid)
 
 
-def cross_kernel(late, *refs):
-    count = 3 if late else 2
-    piece_refs = refs[: 2 * count]
+FAR, NEAR, OWN = 0, 1, 2
+
+
+def cross_kernel(places, *refs):
+    late = (FAR, 0) in places
+    piece_refs = refs[: len(places)]
     if late:
-        table_ref, early_ref, out_ref, held, left, turned, sems = refs[2 * count :]
-        out_ref[...] = early_ref[...]
+        table_ref, early_ref, out_ref, held, left, turned, sems = refs[len(places) :]
+        out_ref[:, :2] = early_ref[...]
     else:
-        table_ref, out_ref, held, left, turned, sems = refs[2 * count :]
+        table_ref, out_ref, held, left, turned, sems = refs[len(places) :]
     core = core_index()
     copies = []
-    for index in range(count):
-        for which in range(2):
-            parity = core if which == 0 else 1 - core
-            start = pl.multiple_of(parity * PIECE, PIECE)
-            copy = pltpu.make_async_copy(
-                piece_refs[2 * index + which],
-                held.at[index, :, pl.ds(start, PIECE), :],
-                sems.at[2 * index + which],
-            )
-            copy.start()
-            copies.append(copy)
+    for index, (chip, other) in enumerate(places):
+        parity = 1 - core if other else core
+        start = pl.multiple_of(parity * PIECE, PIECE)
+        copy = pltpu.make_async_copy(
+            piece_refs[index], held.at[chip, :, pl.ds(start, PIECE), :], sems.at[index]
+        )
+        copy.start()
+        copies.append(copy)
     for copy in copies:
         copy.wait()
-    if late:
-        pairs = ((1, 1 + core, 2 - core), (3, 1 - core, core))
-    else:
-        pairs = ((0, 1, 1), (2, 1 - core, core))
+    pairs = ((OWN, FAR), (NEAR, FAR)) if late else ((OWN, OWN), (NEAR, OWN))
 
     row = lax.broadcasted_iota(jnp.int32, (ROWS, ROWS), 0)
     col = lax.broadcasted_iota(jnp.int32, (ROWS, ROWS), 1)
@@ -120,7 +117,7 @@
     lane = lax.broadcasted_iota(jnp.int32, (16, ROWS), 1)
     sign = jnp.where(lax.broadcasted_iota(jnp.int32, (ROWS, LINES), 1) < WIN, -1.0, 1.0)
 
-    for number, (_, p_side, q_side) in enumerate(pairs):
+    for number, (p_side, q_side) in enumerate(pairs):
         for group in range(GROUPS):
             plain = jnp.dot(
                 swap_rows, held[p_side, group], preferred_element_type=jnp.float32
@@ -131,7 +128,7 @@
 
     for group in range(GROUPS):
         picked = []
-        for number, (_, p_side, q_side) in enumerate(pairs):
+        for number, (p_side, q_side) in enumerate(pairs):
             full = lax.dot_general(
                 left[number, group],
                 held[q_side, group],
@@ -151,8 +148,9 @@
 
     table_high = table_ref[...].astype(jnp.bfloat16)
     table_low = (table_ref[...] - table_high.astype(jnp.float32)).astype(jnp.bfloat16)
-    for first_q in range(0, 16, 4):
-        lines = jnp.concatenate([turned[first_q + step].T for step in range(4)], axis=0)
+    for first_q in range(0, 8, 2):
+        stations = (first_q, first_q + 8, first_q + 1, first_q + 9)
+        lines = jnp.concatenate([turned[q].T for q in stations], axis=0)
         high = lines.astype(jnp.bfloat16)
         low = (lines - high.astype(jnp.float32)).astype(jnp.bfloat16)
         lagged = (
@@ -160,101 +158,97 @@
             + jnp.dot(low, table_high, preferred_element_type=jnp.float32)
             + jnp.dot(high, table_low, preferred_element_type=jnp.float32)
         )
-        for step in range(4):
-            q = first_q + step
-            part = lagged[step * 64 : (step + 1) * 64]
-            summed = part[:32, :LAGS] + part[32:, LAGS:]
-            for number, (apart, _, _) in enumerate(pairs):
+        for step in range(2):
+            sums = []
+            for q_parity in range(2):
+                part = lagged[(2 * step + q_parity) * 64 : (2 * step + q_parity + 1) * 64]
+                sums.append(part[:32, :LAGS] + part[32:, LAGS:])
+            for number in range(2):
                 for parity in range(2):
-                    round_no = 2 * apart + q // 8 - parity
-                    if 0 <= round_no <= ROUNDS:
-                        first = number * 16 + parity * 8
-                        out_ref[parity * 8 + q % 8, round_no] = summed[first : first + 8, :]
+                    cut = slice(number * 16 + parity * 8, number * 16 + parity * 8 + 8)
+                    out_ref[parity * 8 + first_q + step, (2 if late else 0) + number] = (
+                        jnp.concatenate([sums[0][cut], sums[1][cut]], axis=0).astype(
+                            jnp.bfloat16
+                        )
+                    )
 
 
 def cross(pieces, table, early=None):
-    count = len(pieces) // 2
     late = [] if early is None else [early]
+    places = tuple(pieces)
     return pl.pallas_call(
-        lambda *refs: cross_kernel(bool(late), *refs),
-        out_shape=jax.ShapeDtypeStruct((16, ROUNDS + 1, S_DEV, LAGS), jnp.float32),
-        in_specs=[pl.BlockSpec(memory_space=pl.ANY)] * (2 * count)
+        lambda *refs: cross_kernel(places, *refs),
+        out_shape=jax.ShapeDtypeStruct((16, 4 if late else 2, 16, LAGS), jnp.bfloat16),
+        in_specs=[pl.BlockSpec(memory_space=pl.ANY)] * len(places)
         + [pl.BlockSpec(memory_space=pltpu.VMEM)] * (1 + len(late)),
         out_specs=pl.BlockSpec(memory_space=pltpu.VMEM),
         scratch_shapes=[
-            pltpu.VMEM((count, GROUPS, ROWS, LINES), jnp.bfloat16),
+            pltpu.VMEM((3, GROUPS, ROWS, LINES), jnp.bfloat16),
             pltpu.VMEM((2, GROUPS, 2 * ROWS, LINES), jnp.bfloat16),
             pltpu.VMEM((16, BAND_BINS, 64), jnp.float32),
-            pltpu.SemaphoreType.DMA((2 * count,)),
+            pltpu.SemaphoreType.DMA((len(places),)),
         ],
         compiler_params=pltpu.CompilerParams(vmem_limit_bytes=VMEM_LIMIT),
         cost_estimate=pl.CostEstimate(
             flops=2 * 2 * GROUPS * 3 * ROWS * ROWS * LINES,
-            bytes_accessed=count * 524288 + 262144,
+            bytes_accessed=len(places) * 262144 + 262144,
             transcendentals=0,
         ),
-    )(*pieces, table, *late)
-
-
-def gather_kernel(parts_ref, home_ref, one_ref, two_ref, slots):
-    core = core_index()
-    for half in range(2):
-        total = parts_ref[half * 8]
-        for index in range(1, 8):
-            total = total + parts_ref[half * 8 + index]
-        slots[half, pl.ds(core, ROUNDS + 1)] = total
-        slots[half, 7 - 7 * core] = jnp.zeros((S_DEV, LAGS), jnp.float32)
-    home_ref[0:2] = slots[0, 0:2] + slots[1, 0:2]
-    home_ref[2:4] = slots[1, 2:4]
-    home_ref[4:6] = slots[0, 4:6]
-    one_ref[0:2] = slots[0, 2:4]
-    one_ref[2:4] = slots[0, 6:8]
-    two_ref[...] = slots[1, 4:8]
+    )(*pieces.values(), table, *late)
+
+
+def gather_kernel(parts_ref, home_ref, away_ref):
+    total = parts_ref[0].astype(jnp.float32)
+    for index in range(1, 16):
+        total = total + parts_ref[index].astype(jnp.float32)
+    home_ref[0] = total[0]
+    home_ref[1] = total[2]
+    away_ref[0] = total[1]
+    away_ref[1] = total[3]
 
 
 def gather(parts):
-    def shape(count):
-        return jax.ShapeDtypeStruct((count, S_DEV, LAGS), jnp.float32)
-
+    half = jax.ShapeDtypeStruct((2, 16, LAGS), jnp.float32)
     return pl.pallas_call(
         gather_kernel,
-        out_shape=(shape(6), shape(4), shape(4)),
-        scratch_shapes=[pltpu.VMEM((2, 8, S_DEV, LAGS), jnp.float32)],
+        out_shape=(half, half),
         compiler_params=pltpu.CompilerParams(vmem_limit_bytes=VMEM_LIMIT),
     )(parts)
 
 
-def finish_kernel(home_ref, one_ref, two_ref, out_ref, slots):
+def finish_kernel(home_ref, away_ref, out_ref, slots):
     core = core_index()
     band = lax.axis_index("band")
     scale = 1.0 / (math.sqrt(WIN) * math.sqrt(NBINS))
-    slots[0:2] = home_ref[0:2]
-    slots[2:4] = home_ref[2:4] + one_ref[0:2]
-    slots[4:6] = home_ref[4:6] + two_ref[0:2]
-    slots[6:8] = one_ref[2:4] + two_ref[2:4]
+    slots[0:16] = home_ref[0]
+    slots[16:32] = away_ref[0]
+    slots[32:48] = home_ref[1]
+    slots[48:64] = away_ref[1]
     for round_no in range(ROUNDS + 1):
-        value = slots[round_no + core] * scale
+        first = pl.multiple_of((round_no + core) * S_DEV, S_DEV)
+        value = slots[pl.ds(first, S_DEV), :] * scale
         if round_no == 0:
             row = lax.broadcasted_iota(jnp.int32, (S_DEV, LAGS), 0)
             value = jnp.where(row == band, 0.0, value)
         out_ref[round_no] = value
 
 
-def finish(home, one, two):
+def finish(home, away):
     return pl.pallas_call(
         finish_kernel,
         out_shape=jax.ShapeDtypeStruct((ROUNDS + 1, S_DEV, LAGS), jnp.float32),
-        scratch_shapes=[pltpu.VMEM((8, S_DEV, LAGS), jnp.float32)],
+        scratch_shapes=[pltpu.VMEM((8 * S_DEV, LAGS), jnp.float32)],
         compiler_params=pltpu.CompilerParams(vmem_limit_bytes=VMEM_LIMIT),
-    )(home, one, two)
-
-
-def send(value, steps, other=False):
+    )(home, away)
+
+
+def send(value, chips, other=False):
     count = lax.axis_size("pair")
     pairs = []
     for source in range(count):
-        core = source % 2
-        target = source - core + 2 * steps[core] + (1 - core if other else core)
+        target = source + 2 * chips
+        if other:
+            target = target + 1 - 2 * (source % 2)
         pairs.append((source, target % count))
     return lax.ppermute(value, "pair", pairs)
 
@@ -282,15 +276,18 @@
     far_same, far_other, own_same, own_other, near_same, near_other = whiten(spectra, validity.T)
     first_bin = (lax.axis_index("band") * 2 + core_index()) * BAND_BINS
     table = lag_table(first_bin)
-    far = [send(far_same, (-2, 2)), send(far_other, (2, -2), other=True)]
-    own = [own_same, send(own_other, (0, 0), other=True)]
-    near = [send(near_same, (1, -1)), send(near_other, (-1, 1), other=True)]
-    early = cross(far + own, table)
-    late = cross(far + near + own, table, early)
-    home, one, two = gather(exchange(late))
-    one = send(one, (-1, -1))
-    two = send(two, (-2, -2))
-    return finish(home, one, two).reshape(ROUNDS + 1, S_DEV, 1, LAGS)
+    pieces = {
+        (FAR, 0): send(far_same, -2),
+        (NEAR, 0): send(near_same, 1),
+        (FAR, 1): send(far_other, -2, other=True),
+        (NEAR, 1): send(near_other, 1, other=True),
+        (OWN, 0): own_same,
+        (OWN, 1): send(own_other, 0, other=True),
+    }
+    early = cross({place: piece for place, piece in pieces.items() if place[0] != FAR}, table)
+    late = cross(pieces, table, early)
+    home, away = gather(exchange(late))
+    return finish(home, send(away, -1)).reshape(ROUNDS + 1, S_DEV, 1, LAGS)
 
 
 def solution(mesh):

time: 65.9 us -> 61.4 us (0.932)
  the two profiles are of different devices: /device:TPU:2 before, /device:TPU:1 now
where the time goes in v3:
time: 61.4 us; the launch traced here: 61 us
  starting transfers between devices  29.9 us (49%)
  blocking collectives  15.5 us (25%)
  waiting for transfers between devices  7.9 us (13%)
  Pallas kernels  6.5 us (11%)
  local copies, waits for them, and re-layouts  0.69 us (1%)
    ppermute x6, starting transfers between devices, send(): return lax.ppermute(value, 'pair', pairs)  29.9 us
    all_to_all x1, blocking collectives, exchange(): lax.all_to_all(value, ('pair', 'band'), 0, 0, tiled=True, axis_index_grou...  15.5 us
    ppermute x6, waiting for transfers between devices, send(): return lax.ppermute(value, 'pair', pairs)  7.9 us
    pallas_call x2, Pallas kernels, cross(): pl.pallas_call(lambda *refs: cross_kernel(places, *refs), out_shape=jax.S...  3.96 us
    pallas_call x1, Pallas kernels, whiten(): pl.pallas_call(whiten_kernel, out_shape=(piece,) * 6, in_specs=[pl.BlockS...  1.88 us
  transfers between devices with their start and end apart: 6, of which 3 were waited for; matrix products, arithmetic and copies ran while one was open for 1% of the time, Pallas kernels for 3%

profile of v3, /device:TPU:1, one launch (start us, length us, event | category | flops | bytes accessed | tf_op | source)
XLA Modules:
  0.0 61.0 jit_solution(9519676837284419150)
XLA Ops:
  0.0 0.0 copy-start
  0.0 0.7 %copy-done = s32[64,8]{0,1:T(8,128)S(1)} copy-done((s32[64,8]{0,1:T(8,128)S(1)}, s32[64,8]{0,1:T(8,128)}, u32[]{:S(2)}) %copy-start) | copy-done | bytes 2072
  0.7 1.9 %shard_map.28 = (bf16[16,64,128]{2,1,0:T(8,128)(2,1)S(1)}, bf16[16,64,128]{2,1,0:T(8,128)(2,1)S(1)}, bf16[16,64,128]{2,1,0:T(8,128)(2,1)S(1)}, bf16[16,64,128]{2...) custom-call(bf16[2,64,8,256]{3,2,1,0:T(8,128)(2,1)} %spectra_hbm.1, ...), custom_call_target="tpu_custom_call" | custom-call | tf_op jit(solution)/shard_map/pallas_call | solution.py:74
  2.6 13.3 %collective-permute-start = (bf16[16,64,128]{2,1,0:T(8,128)(2,1)S(1)}, bf16[16,64,128]{2,1,0:T(8,128)(2,1)S(1)}, u32[]{:S(2)}, u32[]{:S(2)}) collective-permute-start(bf16[16,64,128]{2,1,0:T(8,128)(2,1)S(1)} %get-tuple-element.13), channel_id=1, source_target_pairs={{0,480},{8,488},{16,496},{24,504},{32,0},{40,8},{48,16},{56,24},{6... | collective-permute-start | bytes 786440 | tf_op jit(solution)/shard_map/ppermute | solution.py:253
  15.9 2.6 %collective-permute-start.1 = (bf16[16,64,128]{2,1,0:T(8,128)(2,1)S(1)}, bf16[16,64,128]{2,1,0:T(8,128)(2,1)S(1)}, u32[]{:S(2)}, u32[]{:S(2)}) collective-permute-start(bf16[16,64,128]{2,1,0:T(8,128)(2,1)S(1)} %get-tuple-element.14), channel_id=1, source_target_pairs={{0,16},{8,24},{16,32},{24,40},{32,48},{40,56},{48,64},{56,72},{64,... | collective-permute-start | bytes 786440 | tf_op jit(solution)/shard_map/ppermute | solution.py:253
  18.6 4.2 %collective-permute-start.2 = (bf16[16,64,128]{2,1,0:T(8,128)(2,1)S(1)}, bf16[16,64,128]{2,1,0:T(8,128)(2,1)S(1)}, u32[]{:S(2)}, u32[]{:S(2)}) collective-permute-start(bf16[16,64,128]{2,1,0:T(8,128)(2,1)S(1)} %get-tuple-element.15), channel_id=1, source_target_pairs={{0,488},{8,480},{16,504},{24,496},{32,8},{40,0},{48,24},{56,16},{6... | collective-permute-start | bytes 786440 | tf_op jit(solution)/shard_map/ppermute | solution.py:253
  22.8 3.9 %collective-permute-start.3 = (bf16[16,64,128]{2,1,0:T(8,128)(2,1)S(1)}, bf16[16,64,128]{2,1,0:T(8,128)(2,1)S(1)}, u32[]{:S(2)}, u32[]{:S(2)}) collective-permute-start(bf16[16,64,128]{2,1,0:T(8,128)(2,1)S(1)} %get-tuple-element.16), channel_id=1, source_target_pairs={{0,24},{8,16},{16,40},{24,32},{32,56},{40,48},{48,72},{56,64},{64,... | collective-permute-start | bytes 786440 | tf_op jit(solution)/shard_map/ppermute | solution.py:253
  26.7 3.1 %collective-permute-start.4 = (bf16[16,64,128]{2,1,0:T(8,128)(2,1)S(1)}, bf16[16,64,128]{2,1,0:T(8,128)(2,1)S(1)}, u32[]{:S(2)}, u32[]{:S(2)}) collective-permute-start(bf16[16,64,128]{2,1,0:T(8,128)(2,1)S(1)} %get-tuple-element.18), channel_id=1, source_target_pairs={{0,8},{8,0},{16,24},{24,16},{32,40},{40,32},{48,56},{56,48},{64,72... | collective-permute-start | bytes 786440 | tf_op jit(solution)/shard_map/ppermute | solution.py:253
  29.9 0.3 fusion.3
  30.2 0.0 collective-permute-done.1.refs_0_.refs_1_
  30.2 3.7 %collective-permute-done.3.refs_1_.refs_3_ = bf16[16,64,128]{2,1,0:T(8,128)(2,1)S(1)} collective-permute-done((bf16[16,64,128]{2,1,0:T(8,128)(2,1)S(1)}, bf16[16,64,128]{2,1,0:T(8,128)(2,1)S(1)}, u32[]{:S(2)}, u32[]{:S(2)}) %collective-permute-start.3) | collective-permute-done | bytes 262176 | tf_op jit(solution)/shard_map/ppermute | solution.py:253
  34.0 0.0 collective-permute-done.4.refs_3_.refs_5_
  34.0 1.9 %shard_map.29.refs_7_ = bf16[16,2,16,128]{3,2,1,0:T(8,128)(2,1)S(1)} custom-call(bf16[16,64,128]{2,1,0:T(8,128)(2,1)S(1)} %collective-permute-done.1.refs_0_.refs_1_, bf16[16,64,128]{2,1,0:T(8,128)(2,1)S(1)} %collective-permute-done.3.refs_1_.refs_3_, bf16[16,64,128]{2,1,0:T(8,128)(2,1)S(1)} %get-tuple-element.17.refs_2_.refs_4_, ...), custom_call_target="tpu_custom_call" | custom-call | flops 402653184 | bytes 1310720 | tf_op jit(solution)/shard_map/pallas_call | solution.py:179
  35.9 0.0 collective-permute-done.refs_0_
  35.9 2.3 %collective-permute-done.2.refs_2_ = bf16[16,64,128]{2,1,0:T(8,128)(2,1)S(1)} collective-permute-done((bf16[16,64,128]{2,1,0:T(8,128)(2,1)S(1)}, bf16[16,64,128]{2,1,0:T(8,128)(2,1)S(1)}, u32[]{:S(2)}, u32[]{:S(2)}) %collective-permute-start.2) | collective-permute-done | bytes 262176 | tf_op jit(solution)/shard_map/ppermute | solution.py:253
  38.3 2.0 %shard_map.30 = bf16[16,4,16,128]{3,2,1,0:T(8,128)(2,1)S(1)} custom-call(bf16[16,64,128]{2,1,0:T(8,128)(2,1)S(1)} %collective-permute-done.refs_0_, bf16[16,64,128]{2,1,0:T(8,128)(2,1)S(1)} %collective-permute-done.1.refs_0_.refs_1_, bf16[16,64,128]{2,1,0:T(8,128)(2,1)S(1)} %collective-permute-done.2.refs_2_, ...), custom_call_target="tpu_custom_call" | custom-call | flops 402653184 | bytes 1835008 | tf_op jit(solution)/shard_map/pallas_call | solution.py:179
  40.3 15.5 %all_to_all.5.parts_ref = bf16[16,4,16,128]{3,2,1,0:T(8,128)(2,1)S(1)} all-to-all(bf16[16,4,16,128]{3,2,1,0:T(8,128)(2,1)S(1)} %shard_map.30), channel_id=1, replica_groups={{0,1,2,3,4,5,6,7,8,9,10,11,12,13,14,15},{16,17,18,19,20,21,22,23,24,25,..., dimensions={0} | all-to-all | bytes 524288 | tf_op jit(solution)/shard_map/all_to_all | solution.py:262
  55.9 2.7 %collective-permute-start.5 = (f32[2,16,128]{2,1,0:T(8,128)S(1)}, f32[2,16,128]{2,1,0:T(8,128)S(1)}, u32[]{:S(2)}, u32[]{:S(2)}) collective-permute-start(f32[2,16,128]{2,1,0:T(8,128)S(1)} %get-tuple-element.20), channel_id=1, source_target_pairs={{0,496},{8,504},{16,0},{24,8},{32,16},{40,24},{48,32},{56,40},{64,... | collective-permute-start | bytes 49160 | tf_op jit(solution)/shard_map/ppermute | solution.py:253
  58.5 1.8 %collective-permute-done.5.away_ref = f32[2,16,128]{2,1,0:T(8,128)S(1)} collective-permute-done((f32[2,16,128]{2,1,0:T(8,128)S(1)}, f32[2,16,128]{2,1,0:T(8,128)S(1)}, u32[]{:S(2)}, u32[]{:S(2)}) %collective-permute-start.5) | collective-permute-done | bytes 16416 | tf_op jit(solution)/shard_map/ppermute | solution.py:253
  60.3 0.6 %shard_map.32 = f32[7,8,128]{2,1,0:T(8,128)} custom-call(f32[2,16,128]{2,1,0:T(8,128)S(1)} %get-tuple-element.19.home_ref, f32[2,16,128]{2,1,0:T(8,128)S(1)} %collective-permute-done.5.away_ref), custom_call_target="tpu_custom_call" | custom-call | tf_op jit(solution)/shard_map/pallas_call | solution.py:237
  (3 shorter events, 0.1 us)
Async XLA Ops:
  0.0 0.7 %copy-start = (s32[64,8]{0,1:T(8,128)S(1)}, s32[64,8]{0,1:T(8,128)}, u32[]{:S(2)}) copy-start(s32[64,8]{0,1:T(8,128)} %param.3) | copy-start | bytes 6148
  2.6 33.3 %collective-permute-start = (bf16[16,64,128]{2,1,0:T(8,128)(2,1)S(1)}, bf16[16,64,128]{2,1,0:T(8,128)(2,1)S(1)}, u32[]{:S(2)}, u32[]{:S(2)}) collective-permute-start(bf16[16,64,128]{2,1,0:T(8,128)(2,1)S(1)} %get-tuple-element.13), channel_id=1, source_target_pairs={{0,480},{8,488},{16,496},{24,504},{32,0},{40,8},{48,16},{56,24},{6... | collective-permute-start | bytes 786440 | tf_op jit(solution)/shard_map/ppermute | solution.py:253
  15.9 14.3 %collective-permute-start.1 = (bf16[16,64,128]{2,1,0:T(8,128)(2,1)S(1)}, bf16[16,64,128]{2,1,0:T(8,128)(2,1)S(1)}, u32[]{:S(2)}, u32[]{:S(2)}) collective-permute-start(bf16[16,64,128]{2,1,0:T(8,128)(2,1)S(1)} %get-tuple-element.14), channel_id=1, source_target_pairs={{0,16},{8,24},{16,32},{24,40},{32,48},{40,56},{48,64},{56,72},{64,... | collective-permute-start | bytes 786440 | tf_op jit(solution)/shard_map/ppermute | solution.py:253
  18.6 19.7 %collective-permute-start.2 = (bf16[16,64,128]{2,1,0:T(8,128)(2,1)S(1)}, bf16[16,64,128]{2,1,0:T(8,128)(2,1)S(1)}, u32[]{:S(2)}, u32[]{:S(2)}) collective-permute-start(bf16[16,64,128]{2,1,0:T(8,128)(2,1)S(1)} %get-tuple-element.15), channel_id=1, source_target_pairs={{0,488},{8,480},{16,504},{24,496},{32,8},{40,0},{48,24},{56,16},{6... | collective-permute-start | bytes 786440 | tf_op jit(solution)/shard_map/ppermute | solution.py:253
  22.8 11.2 %collective-permute-start.3 = (bf16[16,64,128]{2,1,0:T(8,128)(2,1)S(1)}, bf16[16,64,128]{2,1,0:T(8,128)(2,1)S(1)}, u32[]{:S(2)}, u32[]{:S(2)}) collective-permute-start(bf16[16,64,128]{2,1,0:T(8,128)(2,1)S(1)} %get-tuple-element.16), channel_id=1, source_target_pairs={{0,24},{8,16},{16,40},{24,32},{32,56},{40,48},{48,72},{56,64},{64,... | collective-permute-start | bytes 786440 | tf_op jit(solution)/shard_map/ppermute | solution.py:253
  26.7 7.3 %collective-permute-start.4 = (bf16[16,64,128]{2,1,0:T(8,128)(2,1)S(1)}, bf16[16,64,128]{2,1,0:T(8,128)(2,1)S(1)}, u32[]{:S(2)}, u32[]{:S(2)}) collective-permute-start(bf16[16,64,128]{2,1,0:T(8,128)(2,1)S(1)} %get-tuple-element.18), channel_id=1, source_target_pairs={{0,8},{8,0},{16,24},{24,16},{32,40},{40,32},{48,56},{56,48},{64,72... | collective-permute-start | bytes 786440 | tf_op jit(solution)/shard_map/ppermute | solution.py:253
  55.9 4.5 %collective-permute-start.5 = (f32[2,16,128]{2,1,0:T(8,128)S(1)}, f32[2,16,128]{2,1,0:T(8,128)S(1)}, u32[]{:S(2)}, u32[]{:S(2)}) collective-permute-start(f32[2,16,128]{2,1,0:T(8,128)S(1)} %get-tuple-element.20), channel_id=1, source_target_pairs={{0,496},{8,504},{16,0},{24,8},{32,16},{40,24},{48,32},{56,40},{64,... | collective-permute-start | bytes 49160 | tf_op jit(solution)/shard_map/ppermute | solution.py:253

commit v4 on v3

--- a/solution.py
+++ b/solution.py
@@ -18,9 +18,9 @@
 GROUPS = BAND_BINS // GROUP
 PIECE = S_DEV * GROUP
 ROWS = 2 * PIECE
-CHUNKS = 4
+CHUNKS = 2
 WHITEN_LIMIT = 52 * 1024 * 1024
-VMEM_LIMIT = 48 * 1024 * 1024
+VMEM_LIMIT = 24 * 1024 * 1024
 
 
 def core_index():
@@ -93,13 +93,15 @@
     late = (FAR, 0) in places
     piece_refs = refs[: len(places)]
     if late:
-        table_ref, early_ref, out_ref, held, left, turned, sems = refs[len(places) :]
+        table_ref, early_ref, left, out_ref, held, turned, sems = refs[len(places) :]
         out_ref[:, :2] = early_ref[...]
     else:
-        table_ref, out_ref, held, left, turned, sems = refs[len(places) :]
+        table_ref, out_ref, left, held, turned, sems = refs[len(places) :]
     core = core_index()
     copies = []
     for index, (chip, other) in enumerate(places):
+        if late and chip != FAR:
+            continue
         parity = 1 - core if other else core
         start = pl.multiple_of(parity * PIECE, PIECE)
         copy = pltpu.make_async_copy(
@@ -117,7 +119,7 @@
     lane = lax.broadcasted_iota(jnp.int32, (16, ROWS), 1)
     sign = jnp.where(lax.broadcasted_iota(jnp.int32, (ROWS, LINES), 1) < WIN, -1.0, 1.0)
 
-    for number, (p_side, q_side) in enumerate(pairs):
+    for number, (p_side, q_side) in enumerate(() if late else pairs):
         for group in range(GROUPS):
             plain = jnp.dot(
                 swap_rows, held[p_side, group], preferred_element_type=jnp.float32
@@ -173,18 +175,17 @@
                     )
 
 
-def cross(pieces, table, early=None):
-    late = [] if early is None else [early]
+def cross(pieces, table, *early):
     places = tuple(pieces)
+    shape = jax.ShapeDtypeStruct((16, 4 if early else 2, 16, LAGS), jnp.bfloat16)
+    left = jax.ShapeDtypeStruct((2, GROUPS, 2 * ROWS, LINES), jnp.bfloat16)
     return pl.pallas_call(
         lambda *refs: cross_kernel(places, *refs),
-        out_shape=jax.ShapeDtypeStruct((16, 4 if late else 2, 16, LAGS), jnp.bfloat16),
+        out_shape=shape if early else (shape, left),
         in_specs=[pl.BlockSpec(memory_space=pl.ANY)] * len(places)
-        + [pl.BlockSpec(memory_space=pltpu.VMEM)] * (1 + len(late)),
-        out_specs=pl.BlockSpec(memory_space=pltpu.VMEM),
+        + [pl.BlockSpec(memory_space=pltpu.VMEM)] * (1 + len(early)),
         scratch_shapes=[
             pltpu.VMEM((3, GROUPS, ROWS, LINES), jnp.bfloat16),
-            pltpu.VMEM((2, GROUPS, 2 * ROWS, LINES), jnp.bfloat16),
             pltpu.VMEM((16, BAND_BINS, 64), jnp.float32),
             pltpu.SemaphoreType.DMA((len(places),)),
         ],
@@ -194,7 +195,7 @@
             bytes_accessed=len(places) * 262144 + 262144,
             transcendentals=0,
         ),
-    )(*pieces.values(), table, *late)
+    )(*pieces.values(), table, *early)
 
 
 def gather_kernel(parts_ref, home_ref, away_ref):
@@ -276,16 +277,16 @@
     far_same, far_other, own_same, own_other, near_same, near_other = whiten(spectra, validity.T)
     first_bin = (lax.axis_index("band") * 2 + core_index()) * BAND_BINS
     table = lag_table(first_bin)
-    pieces = {
-        (FAR, 0): send(far_same, -2),
-        (NEAR, 0): send(near_same, 1),
-        (FAR, 1): send(far_other, -2, other=True),
+    first = {(FAR, 0): send(far_same, -2)}
+    middle = {(NEAR, 0): send(near_same, 1)}
+    second = {(FAR, 1): send(far_other, -2, other=True)}
+    last = {
         (NEAR, 1): send(near_other, 1, other=True),
         (OWN, 0): own_same,
         (OWN, 1): send(own_other, 0, other=True),
     }
-    early = cross({place: piece for place, piece in pieces.items() if place[0] != FAR}, table)
-    late = cross(pieces, table, early)
+    early = cross(middle | last, table)
+    late = cross(first | middle | second, table, *early)
     home, away = gather(exchange(late))
     return finish(home, send(away, -1)).reshape(ROUNDS + 1, S_DEV, 1, LAGS)
 

time: 61.4 us -> 60.8 us (level)
  Pallas kernels: 6.5 us -> 5.87 us
where the time goes in v4:
time: 60.8 us; the launch traced here: 60.3 us
  starting transfers between devices  29.9 us (49%)
  blocking collectives  15.5 us (25%)
  waiting for transfers between devices  7.88 us (13%)
  Pallas kernels  5.87 us (10%)
  local copies, waits for them, and re-layouts  0.69 us (1%)
    ppermute x6, starting transfers between devices, send(): return lax.ppermute(value, 'pair', pairs)  29.9 us
    all_to_all x1, blocking collectives, exchange(): lax.all_to_all(value, ('pair', 'band'), 0, 0, tiled=True, axis_index_grou...  15.5 us
    ppermute x6, waiting for transfers between devices, send(): return lax.ppermute(value, 'pair', pairs)  7.88 us
    pallas_call x2, Pallas kernels, cross(): pl.pallas_call(lambda *refs: cross_kernel(places, *refs), out_shape=shape...  3.47 us
    pallas_call x1, Pallas kernels, whiten(): pl.pallas_call(whiten_kernel, out_shape=(piece,) * 6, in_specs=[pl.BlockS...  1.73 us
  transfers between devices with their start and end apart: 6, of which 3 were waited for; matrix products, arithmetic and copies ran while one was open for 1% of the time, Pallas kernels for 3%

profile of v4, /device:TPU:1, one launch (start us, length us, event | category | flops | bytes accessed | tf_op | source)
XLA Modules:
  0.0 60.3 jit_solution(3517735142711002919)
XLA Ops:
  0.0 0.0 copy-start
  0.0 0.7 %copy-done = s32[64,8]{0,1:T(8,128)S(1)} copy-done((s32[64,8]{0,1:T(8,128)S(1)}, s32[64,8]{0,1:T(8,128)}, u32[]{:S(2)}) %copy-start) | copy-done | bytes 2072
  0.7 1.7 %shard_map.28 = (bf16[16,64,128]{2,1,0:T(8,128)(2,1)S(1)}, bf16[16,64,128]{2,1,0:T(8,128)(2,1)S(1)}, bf16[16,64,128]{2,1,0:T(8,128)(2,1)S(1)}, bf16[16,64,128]{2...) custom-call(bf16[2,64,8,256]{3,2,1,0:T(8,128)(2,1)} %spectra_hbm.1, ...), custom_call_target="tpu_custom_call" | custom-call | tf_op jit(solution)/shard_map/pallas_call | solution.py:74
  2.4 13.3 %collective-permute-start = (bf16[16,64,128]{2,1,0:T(8,128)(2,1)S(1)}, bf16[16,64,128]{2,1,0:T(8,128)(2,1)S(1)}, u32[]{:S(2)}, u32[]{:S(2)}) collective-permute-start(bf16[16,64,128]{2,1,0:T(8,128)(2,1)S(1)} %get-tuple-element.15), channel_id=1, source_target_pairs={{0,480},{8,488},{16,496},{24,504},{32,0},{40,8},{48,16},{56,24},{6... | collective-permute-start | bytes 786440 | tf_op jit(solution)/shard_map/ppermute | solution.py:254
  15.8 2.6 %collective-permute-start.1 = (bf16[16,64,128]{2,1,0:T(8,128)(2,1)S(1)}, bf16[16,64,128]{2,1,0:T(8,128)(2,1)S(1)}, u32[]{:S(2)}, u32[]{:S(2)}) collective-permute-start(bf16[16,64,128]{2,1,0:T(8,128)(2,1)S(1)} %get-tuple-element.16), channel_id=1, source_target_pairs={{0,16},{8,24},{16,32},{24,40},{32,48},{40,56},{48,64},{56,72},{64,... | collective-permute-start | bytes 786440 | tf_op jit(solution)/shard_map/ppermute | solution.py:254
  18.4 4.2 %collective-permute-start.2 = (bf16[16,64,128]{2,1,0:T(8,128)(2,1)S(1)}, bf16[16,64,128]{2,1,0:T(8,128)(2,1)S(1)}, u32[]{:S(2)}, u32[]{:S(2)}) collective-permute-start(bf16[16,64,128]{2,1,0:T(8,128)(2,1)S(1)} %get-tuple-element.17), channel_id=1, source_target_pairs={{0,488},{8,480},{16,504},{24,496},{32,8},{40,0},{48,24},{56,16},{6... | collective-permute-start | bytes 786440 | tf_op jit(solution)/shard_map/ppermute | solution.py:254
  22.6 3.9 %collective-permute-start.3 = (bf16[16,64,128]{2,1,0:T(8,128)(2,1)S(1)}, bf16[16,64,128]{2,1,0:T(8,128)(2,1)S(1)}, u32[]{:S(2)}, u32[]{:S(2)}) collective-permute-start(bf16[16,64,128]{2,1,0:T(8,128)(2,1)S(1)} %get-tuple-element.18), channel_id=1, source_target_pairs={{0,24},{8,16},{16,40},{24,32},{32,56},{40,48},{48,72},{56,64},{64,... | collective-permute-start | bytes 786440 | tf_op jit(solution)/shard_map/ppermute | solution.py:254
  26.5 3.1 %collective-permute-start.4 = (bf16[16,64,128]{2,1,0:T(8,128)(2,1)S(1)}, bf16[16,64,128]{2,1,0:T(8,128)(2,1)S(1)}, u32[]{:S(2)}, u32[]{:S(2)}) collective-permute-start(bf16[16,64,128]{2,1,0:T(8,128)(2,1)S(1)} %get-tuple-element.20), channel_id=1, source_target_pairs={{0,8},{8,0},{16,24},{24,16},{32,40},{40,32},{48,56},{56,48},{64,72... | collective-permute-start | bytes 786440 | tf_op jit(solution)/shard_map/ppermute | solution.py:254
  29.7 0.3 fusion.3
  30.1 0.0 collective-permute-done.1.refs_0_.refs_1_
  30.1 3.7 %collective-permute-done.3.refs_1_ = bf16[16,64,128]{2,1,0:T(8,128)(2,1)S(1)} collective-permute-done((bf16[16,64,128]{2,1,0:T(8,128)(2,1)S(1)}, bf16[16,64,128]{2,1,0:T(8,128)(2,1)S(1)}, u32[]{:S(2)}, u32[]{:S(2)}) %collective-permute-start.3) | collective-permute-done | bytes 262176 | tf_op jit(solution)/shard_map/ppermute | solution.py:254
  33.8 0.0 collective-permute-done.4.refs_3_
  33.8 1.9 %shard_map.29 = (bf16[16,2,16,128]{3,2,1,0:T(8,128)(2,1)S(1)}, bf16[2,16,256,128]{3,2,1,0:T(8,128)(2,1)S(1)}) custom-call(bf16[16,64,128]{2,1,0:T(8,128)(2,1)S(1)} %collective-permute-done.1.refs_0_.refs_1_, bf16[16,64,128]{2,1,0:T(8,128)(2,1)S(1)} %collective-permute-done.3.refs_1_, bf16[16,64,128]{2,1,0:T(8,128)(2,1)S(1)} %get-tuple-element.19.refs_2_, ...), custom_call_target="tpu_custom_call" | custom-call | flops 402653184 | bytes 1310720 | tf_op jit(solution)/shard_map/pallas_call | solution.py:182
  35.8 0.0 collective-permute-done.refs_0_
  35.8 2.3 %collective-permute-done.2.refs_2_ = bf16[16,64,128]{2,1,0:T(8,128)(2,1)S(1)} collective-permute-done((bf16[16,64,128]{2,1,0:T(8,128)(2,1)S(1)}, bf16[16,64,128]{2,1,0:T(8,128)(2,1)S(1)}, u32[]{:S(2)}, u32[]{:S(2)}) %collective-permute-start.2) | collective-permute-done | bytes 262176 | tf_op jit(solution)/shard_map/ppermute | solution.py:254
  38.1 1.5 %shard_map.30 = bf16[16,4,16,128]{3,2,1,0:T(8,128)(2,1)S(1)} custom-call(bf16[16,64,128]{2,1,0:T(8,128)(2,1)S(1)} %collective-permute-done.refs_0_, bf16[16,64,128]{2,1,0:T(8,128)(2,1)S(1)} %collective-permute-done.1.refs_0_.refs_1_, bf16[16,64,128]{2,1,0:T(8,128)(2,1)S(1)} %collective-permute-done.2.refs_2_, ...), custom_call_target="tpu_custom_call" | custom-call | flops 402653184 | bytes 1048576 | tf_op jit(solution)/shard_map/pallas_call | solution.py:182
  39.7 15.5 %all_to_all.5.parts_ref = bf16[16,4,16,128]{3,2,1,0:T(8,128)(2,1)S(1)} all-to-all(bf16[16,4,16,128]{3,2,1,0:T(8,128)(2,1)S(1)} %shard_map.30), channel_id=1, replica_groups={{0,1,2,3,4,5,6,7,8,9,10,11,12,13,14,15},{16,17,18,19,20,21,22,23,24,25,..., dimensions={0} | all-to-all | bytes 524288 | tf_op jit(solution)/shard_map/all_to_all | solution.py:263
  55.2 2.7 %collective-permute-start.5 = (f32[2,16,128]{2,1,0:T(8,128)S(1)}, f32[2,16,128]{2,1,0:T(8,128)S(1)}, u32[]{:S(2)}, u32[]{:S(2)}) collective-permute-start(f32[2,16,128]{2,1,0:T(8,128)S(1)} %get-tuple-element.24), channel_id=1, source_target_pairs={{0,496},{8,504},{16,0},{24,8},{32,16},{40,24},{48,32},{56,40},{64,... | collective-permute-start | bytes 49160 | tf_op jit(solution)/shard_map/ppermute | solution.py:254
  57.9 1.8 %collective-permute-done.5.away_ref = f32[2,16,128]{2,1,0:T(8,128)S(1)} collective-permute-done((f32[2,16,128]{2,1,0:T(8,128)S(1)}, f32[2,16,128]{2,1,0:T(8,128)S(1)}, u32[]{:S(2)}, u32[]{:S(2)}) %collective-permute-start.5) | collective-permute-done | bytes 16416 | tf_op jit(solution)/shard_map/ppermute | solution.py:254
  59.7 0.6 %shard_map.32 = f32[7,8,128]{2,1,0:T(8,128)} custom-call(f32[2,16,128]{2,1,0:T(8,128)S(1)} %get-tuple-element.23.home_ref, f32[2,16,128]{2,1,0:T(8,128)S(1)} %collective-permute-done.5.away_ref), custom_call_target="tpu_custom_call" | custom-call | tf_op jit(solution)/shard_map/pallas_call | solution.py:238
  (3 shorter events, 0.1 us)
Async XLA Ops:
  0.0 0.7 %copy-start = (s32[64,8]{0,1:T(8,128)S(1)}, s32[64,8]{0,1:T(8,128)}, u32[]{:S(2)}) copy-start(s32[64,8]{0,1:T(8,128)} %param.3) | copy-start | bytes 6148
  2.4 33.4 %collective-permute-start = (bf16[16,64,128]{2,1,0:T(8,128)(2,1)S(1)}, bf16[16,64,128]{2,1,0:T(8,128)(2,1)S(1)}, u32[]{:S(2)}, u32[]{:S(2)}) collective-permute-start(bf16[16,64,128]{2,1,0:T(8,128)(2,1)S(1)} %get-tuple-element.15), channel_id=1, source_target_pairs={{0,480},{8,488},{16,496},{24,504},{32,0},{40,8},{48,16},{56,24},{6... | collective-permute-start | bytes 786440 | tf_op jit(solution)/shard_map/ppermute | solution.py:254
  15.8 14.3 %collective-permute-start.1 = (bf16[16,64,128]{2,1,0:T(8,128)(2,1)S(1)}, bf16[16,64,128]{2,1,0:T(8,128)(2,1)S(1)}, u32[]{:S(2)}, u32[]{:S(2)}) collective-permute-start(bf16[16,64,128]{2,1,0:T(8,128)(2,1)S(1)} %get-tuple-element.16), channel_id=1, source_target_pairs={{0,16},{8,24},{16,32},{24,40},{32,48},{40,56},{48,64},{56,72},{64,... | collective-permute-start | bytes 786440 | tf_op jit(solution)/shard_map/ppermute | solution.py:254
  18.4 19.7 %collective-permute-start.2 = (bf16[16,64,128]{2,1,0:T(8,128)(2,1)S(1)}, bf16[16,64,128]{2,1,0:T(8,128)(2,1)S(1)}, u32[]{:S(2)}, u32[]{:S(2)}) collective-permute-start(bf16[16,64,128]{2,1,0:T(8,128)(2,1)S(1)} %get-tuple-element.17), channel_id=1, source_target_pairs={{0,488},{8,480},{16,504},{24,496},{32,8},{40,0},{48,24},{56,16},{6... | collective-permute-start | bytes 786440 | tf_op jit(solution)/shard_map/ppermute | solution.py:254
  22.6 11.2 %collective-permute-start.3 = (bf16[16,64,128]{2,1,0:T(8,128)(2,1)S(1)}, bf16[16,64,128]{2,1,0:T(8,128)(2,1)S(1)}, u32[]{:S(2)}, u32[]{:S(2)}) collective-permute-start(bf16[16,64,128]{2,1,0:T(8,128)(2,1)S(1)} %get-tuple-element.18), channel_id=1, source_target_pairs={{0,24},{8,16},{16,40},{24,32},{32,56},{40,48},{48,72},{56,64},{64,... | collective-permute-start | bytes 786440 | tf_op jit(solution)/shard_map/ppermute | solution.py:254
  26.5 7.3 %collective-permute-start.4 = (bf16[16,64,128]{2,1,0:T(8,128)(2,1)S(1)}, bf16[16,64,128]{2,1,0:T(8,128)(2,1)S(1)}, u32[]{:S(2)}, u32[]{:S(2)}) collective-permute-start(bf16[16,64,128]{2,1,0:T(8,128)(2,1)S(1)} %get-tuple-element.20), channel_id=1, source_target_pairs={{0,8},{8,0},{16,24},{24,16},{32,40},{40,32},{48,56},{56,48},{64,72... | collective-permute-start | bytes 786440 | tf_op jit(solution)/shard_map/ppermute | solution.py:254
  55.2 4.5 %collective-permute-start.5 = (f32[2,16,128]{2,1,0:T(8,128)S(1)}, f32[2,16,128]{2,1,0:T(8,128)S(1)}, u32[]{:S(2)}, u32[]{:S(2)}) collective-permute-start(f32[2,16,128]{2,1,0:T(8,128)S(1)} %get-tuple-element.24), channel_id=1, source_target_pairs={{0,496},{8,504},{16,0},{24,8},{32,16},{40,24},{48,32},{56,40},{64,... | collective-permute-start | bytes 49160 | tf_op jit(solution)/shard_map/ppermute | solution.py:254

commit v5 on v4

--- a/solution.py
+++ b/solution.py
@@ -19,7 +19,6 @@
 PIECE = S_DEV * GROUP
 ROWS = 2 * PIECE
 CHUNKS = 2
-WHITEN_LIMIT = 52 * 1024 * 1024
 VMEM_LIMIT = 24 * 1024 * 1024
 
 
@@ -74,7 +73,7 @@
     return pl.pallas_call(
         whiten_kernel,
         out_shape=(piece,) * 6,
-        in_specs=[pl.BlockSpec(memory_space=pl.ANY)] * 2,
+        in_specs=[pl.BlockSpec(memory_space=pltpu.HBM)] * 2,
         out_specs=[pl.BlockSpec(memory_space=pltpu.VMEM)] * 6,
         scratch_shapes=[
             pltpu.VMEM((2, WIN, S_DEV, 2 * BAND_BINS), jnp.bfloat16),
@@ -82,8 +81,11 @@
             pltpu.VMEM((2, LINES * S_DEV, BAND_BINS), jnp.float32),
             pltpu.SemaphoreType.DMA((CHUNKS + 1,)),
         ],
-        compiler_params=pltpu.CompilerParams(vmem_limit_bytes=WHITEN_LIMIT),
-    )(spectra, valid)
+        compiler_params=pltpu.CompilerParams(vmem_limit_bytes=VMEM_LIMIT),
+    )(
+        pltpu.with_memory_space_constraint(spectra, pltpu.HBM),
+        pltpu.with_memory_space_constraint(valid, pltpu.HBM),
+    )
 
 
 FAR, NEAR, OWN = 0, 1, 2

time: 60.8 us -> 60.1 us (0.988)
  local copies, waits for them, and re-layouts: 0.69 us -> 0 us
    unnamed x2 -> x0, local copies, waits for them, and re-layouts: 0.69 us -> none
where the time goes in v5:
time: 60.1 us; the launch traced here: 59.6 us
  starting transfers between devices  29.9 us (50%)
  blocking collectives  15.5 us (26%)
  waiting for transfers between devices  7.9 us (13%)
  Pallas kernels  5.86 us (10%)
    ppermute x6, starting transfers between devices, send(): return lax.ppermute(value, 'pair', pairs)  29.9 us
    all_to_all x1, blocking collectives, exchange(): lax.all_to_all(value, ('pair', 'band'), 0, 0, tiled=True, axis_index_grou...  15.5 us
    ppermute x6, waiting for transfers between devices, send(): return lax.ppermute(value, 'pair', pairs)  7.9 us
    pallas_call x2, Pallas kernels, cross(): pl.pallas_call(lambda *refs: cross_kernel(places, *refs), out_shape=shape...  3.47 us
    pallas_call x1, Pallas kernels, whiten(): pl.pallas_call(whiten_kernel, out_shape=(piece,) * 6, in_specs=[pl.BlockS...  1.73 us
  transfers between devices with their start and end apart: 6, of which 3 were waited for; matrix products, arithmetic and copies ran while one was open for 1% of the time, Pallas kernels for 3%

profile of v5, /device:TPU:1, one launch (start us, length us, event | category | flops | bytes accessed | tf_op | source)
XLA Modules:
  0.0 59.6 jit_solution(13428009939944644133)
XLA Ops:
  0.0 1.7 %shard_map.28 = (bf16[16,64,128]{2,1,0:T(8,128)(2,1)S(1)}, bf16[16,64,128]{2,1,0:T(8,128)(2,1)S(1)}, bf16[16,64,128]{2,1,0:T(8,128)(2,1)S(1)}, bf16[16,64,128]{2...) custom-call(bf16[2,64,8,256]{3,2,1,0:T(8,128)(2,1)} %spectra_hbm.1, ...), custom_call_target="tpu_custom_call" | custom-call | tf_op jit(solution)/shard_map/pallas_call | solution.py:73
  1.7 13.3 %collective-permute-start = (bf16[16,64,128]{2,1,0:T(8,128)(2,1)S(1)}, bf16[16,64,128]{2,1,0:T(8,128)(2,1)S(1)}, u32[]{:S(2)}, u32[]{:S(2)}) collective-permute-start(bf16[16,64,128]{2,1,0:T(8,128)(2,1)S(1)} %get-tuple-element.15), channel_id=1, source_target_pairs={{0,480},{8,488},{16,496},{24,504},{32,0},{40,8},{48,16},{56,24},{6... | collective-permute-start | bytes 786440 | tf_op jit(solution)/shard_map/ppermute | solution.py:256
  15.1 2.6 %collective-permute-start.1 = (bf16[16,64,128]{2,1,0:T(8,128)(2,1)S(1)}, bf16[16,64,128]{2,1,0:T(8,128)(2,1)S(1)}, u32[]{:S(2)}, u32[]{:S(2)}) collective-permute-start(bf16[16,64,128]{2,1,0:T(8,128)(2,1)S(1)} %get-tuple-element.16), channel_id=1, source_target_pairs={{0,16},{8,24},{16,32},{24,40},{32,48},{40,56},{48,64},{56,72},{64,... | collective-permute-start | bytes 786440 | tf_op jit(solution)/shard_map/ppermute | solution.py:256
  17.7 4.2 %collective-permute-start.2 = (bf16[16,64,128]{2,1,0:T(8,128)(2,1)S(1)}, bf16[16,64,128]{2,1,0:T(8,128)(2,1)S(1)}, u32[]{:S(2)}, u32[]{:S(2)}) collective-permute-start(bf16[16,64,128]{2,1,0:T(8,128)(2,1)S(1)} %get-tuple-element.17), channel_id=1, source_target_pairs={{0,488},{8,480},{16,504},{24,496},{32,8},{40,0},{48,24},{56,16},{6... | collective-permute-start | bytes 786440 | tf_op jit(solution)/shard_map/ppermute | solution.py:256
  21.9 3.9 %collective-permute-start.3 = (bf16[16,64,128]{2,1,0:T(8,128)(2,1)S(1)}, bf16[16,64,128]{2,1,0:T(8,128)(2,1)S(1)}, u32[]{:S(2)}, u32[]{:S(2)}) collective-permute-start(bf16[16,64,128]{2,1,0:T(8,128)(2,1)S(1)} %get-tuple-element.18), channel_id=1, source_target_pairs={{0,24},{8,16},{16,40},{24,32},{32,56},{40,48},{48,72},{56,64},{64,... | collective-permute-start | bytes 786440 | tf_op jit(solution)/shard_map/ppermute | solution.py:256
  25.9 3.1 %collective-permute-start.4 = (bf16[16,64,128]{2,1,0:T(8,128)(2,1)S(1)}, bf16[16,64,128]{2,1,0:T(8,128)(2,1)S(1)}, u32[]{:S(2)}, u32[]{:S(2)}) collective-permute-start(bf16[16,64,128]{2,1,0:T(8,128)(2,1)S(1)} %get-tuple-element.20), channel_id=1, source_target_pairs={{0,8},{8,0},{16,24},{24,16},{32,40},{40,32},{48,56},{56,48},{64,72... | collective-permute-start | bytes 786440 | tf_op jit(solution)/shard_map/ppermute | solution.py:256
  29.0 0.3 fusion.3
  29.4 0.0 collective-permute-done.1.refs_0_.refs_1_
  29.4 3.7 %collective-permute-done.3.refs_1_ = bf16[16,64,128]{2,1,0:T(8,128)(2,1)S(1)} collective-permute-done((bf16[16,64,128]{2,1,0:T(8,128)(2,1)S(1)}, bf16[16,64,128]{2,1,0:T(8,128)(2,1)S(1)}, u32[]{:S(2)}, u32[]{:S(2)}) %collective-permute-start.3) | collective-permute-done | bytes 262176 | tf_op jit(solution)/shard_map/ppermute | solution.py:256
  33.1 0.0 collective-permute-done.4.refs_3_
  33.1 1.9 %shard_map.29 = (bf16[16,2,16,128]{3,2,1,0:T(8,128)(2,1)S(1)}, bf16[2,16,256,128]{3,2,1,0:T(8,128)(2,1)S(1)}) custom-call(bf16[16,64,128]{2,1,0:T(8,128)(2,1)S(1)} %collective-permute-done.1.refs_0_.refs_1_, bf16[16,64,128]{2,1,0:T(8,128)(2,1)S(1)} %collective-permute-done.3.refs_1_, bf16[16,64,128]{2,1,0:T(8,128)(2,1)S(1)} %get-tuple-element.19.refs_2_, ...), custom_call_target="tpu_custom_call" | custom-call | flops 402653184 | bytes 1310720 | tf_op jit(solution)/shard_map/pallas_call | solution.py:184
  35.1 0.0 collective-permute-done.refs_0_
  35.1 2.3 %collective-permute-done.2.refs_2_ = bf16[16,64,128]{2,1,0:T(8,128)(2,1)S(1)} collective-permute-done((bf16[16,64,128]{2,1,0:T(8,128)(2,1)S(1)}, bf16[16,64,128]{2,1,0:T(8,128)(2,1)S(1)}, u32[]{:S(2)}, u32[]{:S(2)}) %collective-permute-start.2) | collective-permute-done | bytes 262176 | tf_op jit(solution)/shard_map/ppermute | solution.py:256
  37.4 1.5 %shard_map.30 = bf16[16,4,16,128]{3,2,1,0:T(8,128)(2,1)S(1)} custom-call(bf16[16,64,128]{2,1,0:T(8,128)(2,1)S(1)} %collective-permute-done.refs_0_, bf16[16,64,128]{2,1,0:T(8,128)(2,1)S(1)} %collective-permute-done.1.refs_0_.refs_1_, bf16[16,64,128]{2,1,0:T(8,128)(2,1)S(1)} %collective-permute-done.2.refs_2_, ...), custom_call_target="tpu_custom_call" | custom-call | flops 402653184 | bytes 1048576 | tf_op jit(solution)/shard_map/pallas_call | solution.py:184
  39.0 15.5 %all_to_all.5.parts_ref = bf16[16,4,16,128]{3,2,1,0:T(8,128)(2,1)S(1)} all-to-all(bf16[16,4,16,128]{3,2,1,0:T(8,128)(2,1)S(1)} %shard_map.30), channel_id=1, replica_groups={{0,1,2,3,4,5,6,7,8,9,10,11,12,13,14,15},{16,17,18,19,20,21,22,23,24,25,..., dimensions={0} | all-to-all | bytes 524288 | tf_op jit(solution)/shard_map/all_to_all | solution.py:265
  54.5 2.7 %collective-permute-start.5 = (f32[2,16,128]{2,1,0:T(8,128)S(1)}, f32[2,16,128]{2,1,0:T(8,128)S(1)}, u32[]{:S(2)}, u32[]{:S(2)}) collective-permute-start(f32[2,16,128]{2,1,0:T(8,128)S(1)} %get-tuple-element.24), channel_id=1, source_target_pairs={{0,496},{8,504},{16,0},{24,8},{32,16},{40,24},{48,32},{56,40},{64,... | collective-permute-start | bytes 49160 | tf_op jit(solution)/shard_map/ppermute | solution.py:256
  57.2 1.8 %collective-permute-done.5.away_ref = f32[2,16,128]{2,1,0:T(8,128)S(1)} collective-permute-done((f32[2,16,128]{2,1,0:T(8,128)S(1)}, f32[2,16,128]{2,1,0:T(8,128)S(1)}, u32[]{:S(2)}, u32[]{:S(2)}) %collective-permute-start.5) | collective-permute-done | bytes 16416 | tf_op jit(solution)/shard_map/ppermute | solution.py:256
  59.0 0.6 %shard_map.32 = f32[7,8,128]{2,1,0:T(8,128)} custom-call(f32[2,16,128]{2,1,0:T(8,128)S(1)} %get-tuple-element.23.home_ref, f32[2,16,128]{2,1,0:T(8,128)S(1)} %collective-permute-done.5.away_ref), custom_call_target="tpu_custom_call" | custom-call | tf_op jit(solution)/shard_map/pallas_call | solution.py:240
  (3 shorter events, 0.1 us)
Async XLA Ops:
  1.7 33.3 %collective-permute-start = (bf16[16,64,128]{2,1,0:T(8,128)(2,1)S(1)}, bf16[16,64,128]{2,1,0:T(8,128)(2,1)S(1)}, u32[]{:S(2)}, u32[]{:S(2)}) collective-permute-start(bf16[16,64,128]{2,1,0:T(8,128)(2,1)S(1)} %get-tuple-element.15), channel_id=1, source_target_pairs={{0,480},{8,488},{16,496},{24,504},{32,0},{40,8},{48,16},{56,24},{6... | collective-permute-start | bytes 786440 | tf_op jit(solution)/shard_map/ppermute | solution.py:256
  15.1 14.3 %collective-permute-start.1 = (bf16[16,64,128]{2,1,0:T(8,128)(2,1)S(1)}, bf16[16,64,128]{2,1,0:T(8,128)(2,1)S(1)}, u32[]{:S(2)}, u32[]{:S(2)}) collective-permute-start(bf16[16,64,128]{2,1,0:T(8,128)(2,1)S(1)} %get-tuple-element.16), channel_id=1, source_target_pairs={{0,16},{8,24},{16,32},{24,40},{32,48},{40,56},{48,64},{56,72},{64,... | collective-permute-start | bytes 786440 | tf_op jit(solution)/shard_map/ppermute | solution.py:256
  17.7 19.7 %collective-permute-start.2 = (bf16[16,64,128]{2,1,0:T(8,128)(2,1)S(1)}, bf16[16,64,128]{2,1,0:T(8,128)(2,1)S(1)}, u32[]{:S(2)}, u32[]{:S(2)}) collective-permute-start(bf16[16,64,128]{2,1,0:T(8,128)(2,1)S(1)} %get-tuple-element.17), channel_id=1, source_target_pairs={{0,488},{8,480},{16,504},{24,496},{32,8},{40,0},{48,24},{56,16},{6... | collective-permute-start | bytes 786440 | tf_op jit(solution)/shard_map/ppermute | solution.py:256
  21.9 11.2 %collective-permute-start.3 = (bf16[16,64,128]{2,1,0:T(8,128)(2,1)S(1)}, bf16[16,64,128]{2,1,0:T(8,128)(2,1)S(1)}, u32[]{:S(2)}, u32[]{:S(2)}) collective-permute-start(bf16[16,64,128]{2,1,0:T(8,128)(2,1)S(1)} %get-tuple-element.18), channel_id=1, source_target_pairs={{0,24},{8,16},{16,40},{24,32},{32,56},{40,48},{48,72},{56,64},{64,... | collective-permute-start | bytes 786440 | tf_op jit(solution)/shard_map/ppermute | solution.py:256
  25.9 7.3 %collective-permute-start.4 = (bf16[16,64,128]{2,1,0:T(8,128)(2,1)S(1)}, bf16[16,64,128]{2,1,0:T(8,128)(2,1)S(1)}, u32[]{:S(2)}, u32[]{:S(2)}) collective-permute-start(bf16[16,64,128]{2,1,0:T(8,128)(2,1)S(1)} %get-tuple-element.20), channel_id=1, source_target_pairs={{0,8},{8,0},{16,24},{24,16},{32,40},{40,32},{48,56},{56,48},{64,72... | collective-permute-start | bytes 786440 | tf_op jit(solution)/shard_map/ppermute | solution.py:256
  54.5 4.5 %collective-permute-start.5 = (f32[2,16,128]{2,1,0:T(8,128)S(1)}, f32[2,16,128]{2,1,0:T(8,128)S(1)}, u32[]{:S(2)}, u32[]{:S(2)}) collective-permute-start(f32[2,16,128]{2,1,0:T(8,128)S(1)} %get-tuple-element.24), channel_id=1, source_target_pairs={{0,496},{8,504},{16,0},{24,8},{32,16},{40,24},{48,32},{56,40},{64,... | collective-permute-start | bytes 49160 | tf_op jit(solution)/shard_map/ppermute | solution.py:256

commit v6 on v5

--- a/solution.py
+++ b/solution.py
@@ -140,8 +140,8 @@
                 preferred_element_type=jnp.float32,
             )
             for part in range(2):
-                total = jnp.zeros((16, ROWS), jnp.float32)
-                for line in range(GROUP):
+                total = full[part * ROWS : part * ROWS + 16, :]
+                for line in range(1, GROUP):
                     first = part * ROWS + line * 16
                     total = jnp.where(
                         lane % GROUP == line, full[first : first + 16, :], total
@@ -154,7 +154,11 @@
     table_low = (table_ref[...] - table_high.astype(jnp.float32)).astype(jnp.bfloat16)
     for first_q in range(0, 8, 2):
         stations = (first_q, first_q + 8, first_q + 1, first_q + 9)
-        lines = jnp.concatenate([turned[q].T for q in stations], axis=0)
+        lines = [turned[q].T for q in stations]
+        lines = jnp.concatenate(
+            [jnp.concatenate([line[part : part + 32] for line in lines], axis=0) for part in (0, 32)],
+            axis=1,
+        )
         high = lines.astype(jnp.bfloat16)
         low = (lines - high.astype(jnp.float32)).astype(jnp.bfloat16)
         lagged = (
@@ -165,8 +169,8 @@
         for step in range(2):
             sums = []
             for q_parity in range(2):
-                part = lagged[(2 * step + q_parity) * 64 : (2 * step + q_parity + 1) * 64]
-                sums.append(part[:32, :LAGS] + part[32:, LAGS:])
+                first = (2 * step + q_parity) * 32
+                sums.append(lagged[first : first + 32])
             for number in range(2):
                 for parity in range(2):
                     cut = slice(number * 16 + parity * 8, number * 16 + parity * 8 + 8)
@@ -272,7 +276,7 @@
     offsets = jnp.arange(LAGS, dtype=jnp.int32) - LAGS // 2
     wrapped = freq[:, None] * offsets[None, :] % (2 * NBINS)
     phase = math.pi * wrapped.astype(jnp.float32) / NBINS
-    return jnp.concatenate([jnp.cos(phase), -jnp.sin(phase)], axis=1)
+    return jnp.concatenate([jnp.cos(phase), -jnp.sin(phase)], axis=0)
 
 
 def body(spectra, validity):

time: 60.1 us -> 59.9 us (level)
  no operation moved by 1% of the time
where the time goes in v6:
time: 59.9 us; the launch traced here: 59.4 us
  starting transfers between devices  29.9 us (50%)
  blocking collectives  15.5 us (26%)
  waiting for transfers between devices  8.08 us (13%)
  Pallas kernels  5.5 us (9%)
    ppermute x6, starting transfers between devices, send(): return lax.ppermute(value, 'pair', pairs)  29.9 us
    all_to_all x1, blocking collectives, exchange(): lax.all_to_all(value, ('pair', 'band'), 0, 0, tiled=True, axis_index_grou...  15.5 us
    ppermute x6, waiting for transfers between devices, send(): return lax.ppermute(value, 'pair', pairs)  8.08 us
    pallas_call x2, Pallas kernels, cross(): pl.pallas_call(lambda *refs: cross_kernel(places, *refs), out_shape=shape...  3.1 us
    pallas_call x1, Pallas kernels, whiten(): pl.pallas_call(whiten_kernel, out_shape=(piece,) * 6, in_specs=[pl.BlockS...  1.73 us
  transfers between devices with their start and end apart: 6, of which 3 were waited for; matrix products, arithmetic and copies ran while one was open for 1% of the time, Pallas kernels for 3%

profile of v6, /device:TPU:1, one launch (start us, length us, event | category | flops | bytes accessed | tf_op | source)
XLA Modules:
  0.0 59.4 jit_solution(12840246440179901996)
XLA Ops:
  0.0 1.7 %shard_map.28 = (bf16[16,64,128]{2,1,0:T(8,128)(2,1)S(1)}, bf16[16,64,128]{2,1,0:T(8,128)(2,1)S(1)}, bf16[16,64,128]{2,1,0:T(8,128)(2,1)S(1)}, bf16[16,64,128]{2...) custom-call(bf16[2,64,8,256]{3,2,1,0:T(8,128)(2,1)} %spectra_hbm.1, ...), custom_call_target="tpu_custom_call" | custom-call | tf_op jit(solution)/shard_map/pallas_call | solution.py:73
  1.7 13.3 %collective-permute-start = (bf16[16,64,128]{2,1,0:T(8,128)(2,1)S(1)}, bf16[16,64,128]{2,1,0:T(8,128)(2,1)S(1)}, u32[]{:S(2)}, u32[]{:S(2)}) collective-permute-start(bf16[16,64,128]{2,1,0:T(8,128)(2,1)S(1)} %get-tuple-element.15), channel_id=1, source_target_pairs={{0,480},{8,488},{16,496},{24,504},{32,0},{40,8},{48,16},{56,24},{6... | collective-permute-start | bytes 786440 | tf_op jit(solution)/shard_map/ppermute | solution.py:260
  15.1 2.6 %collective-permute-start.1 = (bf16[16,64,128]{2,1,0:T(8,128)(2,1)S(1)}, bf16[16,64,128]{2,1,0:T(8,128)(2,1)S(1)}, u32[]{:S(2)}, u32[]{:S(2)}) collective-permute-start(bf16[16,64,128]{2,1,0:T(8,128)(2,1)S(1)} %get-tuple-element.16), channel_id=1, source_target_pairs={{0,16},{8,24},{16,32},{24,40},{32,48},{40,56},{48,64},{56,72},{64,... | collective-permute-start | bytes 786440 | tf_op jit(solution)/shard_map/ppermute | solution.py:260
  17.7 4.2 %collective-permute-start.2 = (bf16[16,64,128]{2,1,0:T(8,128)(2,1)S(1)}, bf16[16,64,128]{2,1,0:T(8,128)(2,1)S(1)}, u32[]{:S(2)}, u32[]{:S(2)}) collective-permute-start(bf16[16,64,128]{2,1,0:T(8,128)(2,1)S(1)} %get-tuple-element.17), channel_id=1, source_target_pairs={{0,488},{8,480},{16,504},{24,496},{32,8},{40,0},{48,24},{56,16},{6... | collective-permute-start | bytes 786440 | tf_op jit(solution)/shard_map/ppermute | solution.py:260
  21.9 3.9 %collective-permute-start.3 = (bf16[16,64,128]{2,1,0:T(8,128)(2,1)S(1)}, bf16[16,64,128]{2,1,0:T(8,128)(2,1)S(1)}, u32[]{:S(2)}, u32[]{:S(2)}) collective-permute-start(bf16[16,64,128]{2,1,0:T(8,128)(2,1)S(1)} %get-tuple-element.18), channel_id=1, source_target_pairs={{0,24},{8,16},{16,40},{24,32},{32,56},{40,48},{48,72},{56,64},{64,... | collective-permute-start | bytes 786440 | tf_op jit(solution)/shard_map/ppermute | solution.py:260
  25.9 3.1 %collective-permute-start.4 = (bf16[16,64,128]{2,1,0:T(8,128)(2,1)S(1)}, bf16[16,64,128]{2,1,0:T(8,128)(2,1)S(1)}, u32[]{:S(2)}, u32[]{:S(2)}) collective-permute-start(bf16[16,64,128]{2,1,0:T(8,128)(2,1)S(1)} %get-tuple-element.20), channel_id=1, source_target_pairs={{0,8},{8,0},{16,24},{24,16},{32,40},{40,32},{48,56},{56,48},{64,72... | collective-permute-start | bytes 786440 | tf_op jit(solution)/shard_map/ppermute | solution.py:260
  29.0 0.3 fusion.3
  29.4 0.0 collective-permute-done.1.refs_0_.refs_1_
  29.4 3.7 %collective-permute-done.3.refs_1_ = bf16[16,64,128]{2,1,0:T(8,128)(2,1)S(1)} collective-permute-done((bf16[16,64,128]{2,1,0:T(8,128)(2,1)S(1)}, bf16[16,64,128]{2,1,0:T(8,128)(2,1)S(1)}, u32[]{:S(2)}, u32[]{:S(2)}) %collective-permute-start.3) | collective-permute-done | bytes 262176 | tf_op jit(solution)/shard_map/ppermute | solution.py:260
  33.1 0.0 collective-permute-done.4.refs_3_
  33.1 1.8 %shard_map.29 = (bf16[16,2,16,128]{3,2,1,0:T(8,128)(2,1)S(1)}, bf16[2,16,256,128]{3,2,1,0:T(8,128)(2,1)S(1)}) custom-call(bf16[16,64,128]{2,1,0:T(8,128)(2,1)S(1)} %collective-permute-done.1.refs_0_.refs_1_, bf16[16,64,128]{2,1,0:T(8,128)(2,1)S(1)} %collective-permute-done.3.refs_1_, bf16[16,64,128]{2,1,0:T(8,128)(2,1)S(1)} %get-tuple-element.19.refs_2_, ...), custom_call_target="tpu_custom_call" | custom-call | flops 402653184 | bytes 1310720 | tf_op jit(solution)/shard_map/pallas_call | solution.py:188
  34.9 0.0 collective-permute-done.refs_0_
  34.9 2.5 %collective-permute-done.2.refs_2_ = bf16[16,64,128]{2,1,0:T(8,128)(2,1)S(1)} collective-permute-done((bf16[16,64,128]{2,1,0:T(8,128)(2,1)S(1)}, bf16[16,64,128]{2,1,0:T(8,128)(2,1)S(1)}, u32[]{:S(2)}, u32[]{:S(2)}) %collective-permute-start.2) | collective-permute-done | bytes 262176 | tf_op jit(solution)/shard_map/ppermute | solution.py:260
  37.4 1.3 %shard_map.30 = bf16[16,4,16,128]{3,2,1,0:T(8,128)(2,1)S(1)} custom-call(bf16[16,64,128]{2,1,0:T(8,128)(2,1)S(1)} %collective-permute-done.refs_0_, bf16[16,64,128]{2,1,0:T(8,128)(2,1)S(1)} %collective-permute-done.1.refs_0_.refs_1_, bf16[16,64,128]{2,1,0:T(8,128)(2,1)S(1)} %collective-permute-done.2.refs_2_, ...), custom_call_target="tpu_custom_call" | custom-call | flops 402653184 | bytes 1048576 | tf_op jit(solution)/shard_map/pallas_call | solution.py:188
  38.8 15.5 %all_to_all.5.parts_ref = bf16[16,4,16,128]{3,2,1,0:T(8,128)(2,1)S(1)} all-to-all(bf16[16,4,16,128]{3,2,1,0:T(8,128)(2,1)S(1)} %shard_map.30), channel_id=1, replica_groups={{0,1,2,3,4,5,6,7,8,9,10,11,12,13,14,15},{16,17,18,19,20,21,22,23,24,25,..., dimensions={0} | all-to-all | bytes 524288 | tf_op jit(solution)/shard_map/all_to_all | solution.py:269
  54.3 2.7 %collective-permute-start.5 = (f32[2,16,128]{2,1,0:T(8,128)S(1)}, f32[2,16,128]{2,1,0:T(8,128)S(1)}, u32[]{:S(2)}, u32[]{:S(2)}) collective-permute-start(f32[2,16,128]{2,1,0:T(8,128)S(1)} %get-tuple-element.24), channel_id=1, source_target_pairs={{0,496},{8,504},{16,0},{24,8},{32,16},{40,24},{48,32},{56,40},{64,... | collective-permute-start | bytes 49160 | tf_op jit(solution)/shard_map/ppermute | solution.py:260
  57.0 1.8 %collective-permute-done.5.away_ref = f32[2,16,128]{2,1,0:T(8,128)S(1)} collective-permute-done((f32[2,16,128]{2,1,0:T(8,128)S(1)}, f32[2,16,128]{2,1,0:T(8,128)S(1)}, u32[]{:S(2)}, u32[]{:S(2)}) %collective-permute-start.5) | collective-permute-done | bytes 16416 | tf_op jit(solution)/shard_map/ppermute | solution.py:260
  58.8 0.6 %shard_map.32 = f32[7,8,128]{2,1,0:T(8,128)} custom-call(f32[2,16,128]{2,1,0:T(8,128)S(1)} %get-tuple-element.23.home_ref, f32[2,16,128]{2,1,0:T(8,128)S(1)} %collective-permute-done.5.away_ref), custom_call_target="tpu_custom_call" | custom-call | tf_op jit(solution)/shard_map/pallas_call | solution.py:244
  (3 shorter events, 0.1 us)
Async XLA Ops:
  1.7 33.2 %collective-permute-start = (bf16[16,64,128]{2,1,0:T(8,128)(2,1)S(1)}, bf16[16,64,128]{2,1,0:T(8,128)(2,1)S(1)}, u32[]{:S(2)}, u32[]{:S(2)}) collective-permute-start(bf16[16,64,128]{2,1,0:T(8,128)(2,1)S(1)} %get-tuple-element.15), channel_id=1, source_target_pairs={{0,480},{8,488},{16,496},{24,504},{32,0},{40,8},{48,16},{56,24},{6... | collective-permute-start | bytes 786440 | tf_op jit(solution)/shard_map/ppermute | solution.py:260
  15.1 14.3 %collective-permute-start.1 = (bf16[16,64,128]{2,1,0:T(8,128)(2,1)S(1)}, bf16[16,64,128]{2,1,0:T(8,128)(2,1)S(1)}, u32[]{:S(2)}, u32[]{:S(2)}) collective-permute-start(bf16[16,64,128]{2,1,0:T(8,128)(2,1)S(1)} %get-tuple-element.16), channel_id=1, source_target_pairs={{0,16},{8,24},{16,32},{24,40},{32,48},{40,56},{48,64},{56,72},{64,... | collective-permute-start | bytes 786440 | tf_op jit(solution)/shard_map/ppermute | solution.py:260
  17.7 19.7 %collective-permute-start.2 = (bf16[16,64,128]{2,1,0:T(8,128)(2,1)S(1)}, bf16[16,64,128]{2,1,0:T(8,128)(2,1)S(1)}, u32[]{:S(2)}, u32[]{:S(2)}) collective-permute-start(bf16[16,64,128]{2,1,0:T(8,128)(2,1)S(1)} %get-tuple-element.17), channel_id=1, source_target_pairs={{0,488},{8,480},{16,504},{24,496},{32,8},{40,0},{48,24},{56,16},{6... | collective-permute-start | bytes 786440 | tf_op jit(solution)/shard_map/ppermute | solution.py:260
  21.9 11.2 %collective-permute-start.3 = (bf16[16,64,128]{2,1,0:T(8,128)(2,1)S(1)}, bf16[16,64,128]{2,1,0:T(8,128)(2,1)S(1)}, u32[]{:S(2)}, u32[]{:S(2)}) collective-permute-start(bf16[16,64,128]{2,1,0:T(8,128)(2,1)S(1)} %get-tuple-element.18), channel_id=1, source_target_pairs={{0,24},{8,16},{16,40},{24,32},{32,56},{40,48},{48,72},{56,64},{64,... | collective-permute-start | bytes 786440 | tf_op jit(solution)/shard_map/ppermute | solution.py:260
  25.9 7.3 %collective-permute-start.4 = (bf16[16,64,128]{2,1,0:T(8,128)(2,1)S(1)}, bf16[16,64,128]{2,1,0:T(8,128)(2,1)S(1)}, u32[]{:S(2)}, u32[]{:S(2)}) collective-permute-start(bf16[16,64,128]{2,1,0:T(8,128)(2,1)S(1)} %get-tuple-element.20), channel_id=1, source_target_pairs={{0,8},{8,0},{16,24},{24,16},{32,40},{40,32},{48,56},{56,48},{64,72... | collective-permute-start | bytes 786440 | tf_op jit(solution)/shard_map/ppermute | solution.py:260
  54.3 4.5 %collective-permute-start.5 = (f32[2,16,128]{2,1,0:T(8,128)S(1)}, f32[2,16,128]{2,1,0:T(8,128)S(1)}, u32[]{:S(2)}, u32[]{:S(2)}) collective-permute-start(f32[2,16,128]{2,1,0:T(8,128)S(1)} %get-tuple-element.24), channel_id=1, source_target_pairs={{0,496},{8,504},{16,0},{24,8},{32,16},{40,24},{48,32},{56,40},{64,... | collective-permute-start | bytes 49160 | tf_op jit(solution)/shard_map/ppermute | solution.py:260

commit v7 on v6

--- a/solution.py
+++ b/solution.py
@@ -102,7 +102,7 @@
     core = core_index()
     copies = []
     for index, (chip, other) in enumerate(places):
-        if late and chip != FAR:
+        if late:
             continue
         parity = 1 - core if other else core
         start = pl.multiple_of(parity * PIECE, PIECE)
@@ -132,10 +132,18 @@
 
     for group in range(GROUPS):
         picked = []
+        if late:
+            mine = piece_refs[places.index((FAR, 0))][group]
+            others = piece_refs[places.index((FAR, 1))][group]
+            right = jnp.concatenate(
+                [jnp.where(core == 0, mine, others), jnp.where(core == 0, others, mine)], axis=0
+            )
+        else:
+            right = held[OWN, group]
         for number, (p_side, q_side) in enumerate(pairs):
             full = lax.dot_general(
                 left[number, group],
-                held[q_side, group],
+                right,
                 (((1,), (1,)), ((), ())),
                 preferred_element_type=jnp.float32,
             )
@@ -188,7 +196,10 @@
     return pl.pallas_call(
         lambda *refs: cross_kernel(places, *refs),
         out_shape=shape if early else (shape, left),
-        in_specs=[pl.BlockSpec(memory_space=pl.ANY)] * len(places)
+        in_specs=[
+            pl.BlockSpec(memory_space=pltpu.VMEM if early and chip == FAR else pl.ANY)
+            for chip, _ in places
+        ]
         + [pl.BlockSpec(memory_space=pltpu.VMEM)] * (1 + len(early)),
         scratch_shapes=[
             pltpu.VMEM((3, GROUPS, ROWS, LINES), jnp.bfloat16),

time: 59.9 us -> 59.9 us (level)
  no operation moved by 1% of the time
where the time goes in v7:
time: 59.9 us; the launch traced here: 59.4 us
  starting transfers between devices  29.9 us (50%)
  blocking collectives  15.5 us (26%)
  waiting for transfers between devices  8.08 us (13%)
  Pallas kernels  5.45 us (9%)
    ppermute x6, starting transfers between devices, send(): return lax.ppermute(value, 'pair', pairs)  29.9 us
    all_to_all x1, blocking collectives, exchange(): lax.all_to_all(value, ('pair', 'band'), 0, 0, tiled=True, axis_index_grou...  15.5 us
    ppermute x6, waiting for transfers between devices, send(): return lax.ppermute(value, 'pair', pairs)  8.08 us
    pallas_call x2, Pallas kernels, cross(): pl.pallas_call(lambda *refs: cross_kernel(places, *refs), out_shape=shape...  3.06 us
    pallas_call x1, Pallas kernels, whiten(): pl.pallas_call(whiten_kernel, out_shape=(piece,) * 6, in_specs=[pl.BlockS...  1.73 us
  transfers between devices with their start and end apart: 6, of which 3 were waited for; matrix products, arithmetic and copies ran while one was open for 1% of the time, Pallas kernels for 3%

profile of v7, /device:TPU:1, one launch (start us, length us, event | category | flops | bytes accessed | tf_op | source)
XLA Modules:
  0.0 59.4 jit_solution(3470845557157579255)
XLA Ops:
  0.0 1.7 %shard_map.28 = (bf16[16,64,128]{2,1,0:T(8,128)(2,1)S(1)}, bf16[16,64,128]{2,1,0:T(8,128)(2,1)S(1)}, bf16[16,64,128]{2,1,0:T(8,128)(2,1)S(1)}, bf16[16,64,128]{2...) custom-call(bf16[2,64,8,256]{3,2,1,0:T(8,128)(2,1)} %spectra_hbm.1, ...), custom_call_target="tpu_custom_call" | custom-call | tf_op jit(solution)/shard_map/pallas_call | solution.py:73
  1.7 13.3 %collective-permute-start = (bf16[16,64,128]{2,1,0:T(8,128)(2,1)S(1)}, bf16[16,64,128]{2,1,0:T(8,128)(2,1)S(1)}, u32[]{:S(2)}, u32[]{:S(2)}) collective-permute-start(bf16[16,64,128]{2,1,0:T(8,128)(2,1)S(1)} %get-tuple-element.15), channel_id=1, source_target_pairs={{0,480},{8,488},{16,496},{24,504},{32,0},{40,8},{48,16},{56,24},{6... | collective-permute-start | bytes 786440 | tf_op jit(solution)/shard_map/ppermute | solution.py:271
  15.1 2.6 %collective-permute-start.1 = (bf16[16,64,128]{2,1,0:T(8,128)(2,1)S(1)}, bf16[16,64,128]{2,1,0:T(8,128)(2,1)S(1)}, u32[]{:S(2)}, u32[]{:S(2)}) collective-permute-start(bf16[16,64,128]{2,1,0:T(8,128)(2,1)S(1)} %get-tuple-element.16), channel_id=1, source_target_pairs={{0,16},{8,24},{16,32},{24,40},{32,48},{40,56},{48,64},{56,72},{64,... | collective-permute-start | bytes 786440 | tf_op jit(solution)/shard_map/ppermute | solution.py:271
  17.7 4.2 %collective-permute-start.2 = (bf16[16,64,128]{2,1,0:T(8,128)(2,1)S(1)}, bf16[16,64,128]{2,1,0:T(8,128)(2,1)S(1)}, u32[]{:S(2)}, u32[]{:S(2)}) collective-permute-start(bf16[16,64,128]{2,1,0:T(8,128)(2,1)S(1)} %get-tuple-element.17), channel_id=1, source_target_pairs={{0,488},{8,480},{16,504},{24,496},{32,8},{40,0},{48,24},{56,16},{6... | collective-permute-start | bytes 786440 | tf_op jit(solution)/shard_map/ppermute | solution.py:271
  21.9 3.9 %collective-permute-start.3 = (bf16[16,64,128]{2,1,0:T(8,128)(2,1)S(1)}, bf16[16,64,128]{2,1,0:T(8,128)(2,1)S(1)}, u32[]{:S(2)}, u32[]{:S(2)}) collective-permute-start(bf16[16,64,128]{2,1,0:T(8,128)(2,1)S(1)} %get-tuple-element.18), channel_id=1, source_target_pairs={{0,24},{8,16},{16,40},{24,32},{32,56},{40,48},{48,72},{56,64},{64,... | collective-permute-start | bytes 786440 | tf_op jit(solution)/shard_map/ppermute | solution.py:271
  25.9 3.1 %collective-permute-start.4 = (bf16[16,64,128]{2,1,0:T(8,128)(2,1)S(1)}, bf16[16,64,128]{2,1,0:T(8,128)(2,1)S(1)}, u32[]{:S(2)}, u32[]{:S(2)}) collective-permute-start(bf16[16,64,128]{2,1,0:T(8,128)(2,1)S(1)} %get-tuple-element.20), channel_id=1, source_target_pairs={{0,8},{8,0},{16,24},{24,16},{32,40},{40,32},{48,56},{56,48},{64,72... | collective-permute-start | bytes 786440 | tf_op jit(solution)/shard_map/ppermute | solution.py:271
  29.0 0.3 fusion.3
  29.4 0.0 collective-permute-done.1.refs_0_.refs_1_
  29.4 3.7 %collective-permute-done.3.refs_1_ = bf16[16,64,128]{2,1,0:T(8,128)(2,1)S(1)} collective-permute-done((bf16[16,64,128]{2,1,0:T(8,128)(2,1)S(1)}, bf16[16,64,128]{2,1,0:T(8,128)(2,1)S(1)}, u32[]{:S(2)}, u32[]{:S(2)}) %collective-permute-start.3) | collective-permute-done | bytes 262176 | tf_op jit(solution)/shard_map/ppermute | solution.py:271
  33.1 0.0 collective-permute-done.4.refs_3_
  33.1 1.8 %shard_map.29 = (bf16[16,2,16,128]{3,2,1,0:T(8,128)(2,1)S(1)}, bf16[2,16,256,128]{3,2,1,0:T(8,128)(2,1)S(1)}) custom-call(bf16[16,64,128]{2,1,0:T(8,128)(2,1)S(1)} %collective-permute-done.1.refs_0_.refs_1_, bf16[16,64,128]{2,1,0:T(8,128)(2,1)S(1)} %collective-permute-done.3.refs_1_, bf16[16,64,128]{2,1,0:T(8,128)(2,1)S(1)} %get-tuple-element.19.refs_2_, ...), custom_call_target="tpu_custom_call" | custom-call | flops 402653184 | bytes 1310720 | tf_op jit(solution)/shard_map/pallas_call | solution.py:196
  34.9 0.0 collective-permute-done.refs_0_
  34.9 2.5 %collective-permute-done.2.refs_2_ = bf16[16,64,128]{2,1,0:T(8,128)(2,1)S(1)} collective-permute-done((bf16[16,64,128]{2,1,0:T(8,128)(2,1)S(1)}, bf16[16,64,128]{2,1,0:T(8,128)(2,1)S(1)}, u32[]{:S(2)}, u32[]{:S(2)}) %collective-permute-start.2) | collective-permute-done | bytes 262176 | tf_op jit(solution)/shard_map/ppermute | solution.py:271
  37.4 1.3 %shard_map.30 = bf16[16,4,16,128]{3,2,1,0:T(8,128)(2,1)S(1)} custom-call(bf16[16,64,128]{2,1,0:T(8,128)(2,1)S(1)} %collective-permute-done.refs_0_, bf16[16,64,128]{2,1,0:T(8,128)(2,1)S(1)} %collective-permute-done.1.refs_0_.refs_1_, bf16[16,64,128]{2,1,0:T(8,128)(2,1)S(1)} %collective-permute-done.2.refs_2_, ...), custom_call_target="tpu_custom_call" | custom-call | flops 402653184 | bytes 1048576 | tf_op jit(solution)/shard_map/pallas_call | solution.py:196
  38.7 15.5 %all_to_all.5.parts_ref = bf16[16,4,16,128]{3,2,1,0:T(8,128)(2,1)S(1)} all-to-all(bf16[16,4,16,128]{3,2,1,0:T(8,128)(2,1)S(1)} %shard_map.30), channel_id=1, replica_groups={{0,1,2,3,4,5,6,7,8,9,10,11,12,13,14,15},{16,17,18,19,20,21,22,23,24,25,..., dimensions={0} | all-to-all | bytes 524288 | tf_op jit(solution)/shard_map/all_to_all | solution.py:280
  54.3 2.6 %collective-permute-start.5 = (f32[2,16,128]{2,1,0:T(8,128)S(1)}, f32[2,16,128]{2,1,0:T(8,128)S(1)}, u32[]{:S(2)}, u32[]{:S(2)}) collective-permute-start(f32[2,16,128]{2,1,0:T(8,128)S(1)} %get-tuple-element.24), channel_id=1, source_target_pairs={{0,496},{8,504},{16,0},{24,8},{32,16},{40,24},{48,32},{56,40},{64,... | collective-permute-start | bytes 49160 | tf_op jit(solution)/shard_map/ppermute | solution.py:271
  57.0 1.8 %collective-permute-done.5.away_ref = f32[2,16,128]{2,1,0:T(8,128)S(1)} collective-permute-done((f32[2,16,128]{2,1,0:T(8,128)S(1)}, f32[2,16,128]{2,1,0:T(8,128)S(1)}, u32[]{:S(2)}, u32[]{:S(2)}) %collective-permute-start.5) | collective-permute-done | bytes 16416 | tf_op jit(solution)/shard_map/ppermute | solution.py:271
  58.8 0.6 %shard_map.32 = f32[7,8,128]{2,1,0:T(8,128)} custom-call(f32[2,16,128]{2,1,0:T(8,128)S(1)} %get-tuple-element.23.home_ref, f32[2,16,128]{2,1,0:T(8,128)S(1)} %collective-permute-done.5.away_ref), custom_call_target="tpu_custom_call" | custom-call | tf_op jit(solution)/shard_map/pallas_call | solution.py:255
  (3 shorter events, 0.1 us)
Async XLA Ops:
  1.7 33.2 %collective-permute-start = (bf16[16,64,128]{2,1,0:T(8,128)(2,1)S(1)}, bf16[16,64,128]{2,1,0:T(8,128)(2,1)S(1)}, u32[]{:S(2)}, u32[]{:S(2)}) collective-permute-start(bf16[16,64,128]{2,1,0:T(8,128)(2,1)S(1)} %get-tuple-element.15), channel_id=1, source_target_pairs={{0,480},{8,488},{16,496},{24,504},{32,0},{40,8},{48,16},{56,24},{6... | collective-permute-start | bytes 786440 | tf_op jit(solution)/shard_map/ppermute | solution.py:271
  15.1 14.3 %collective-permute-start.1 = (bf16[16,64,128]{2,1,0:T(8,128)(2,1)S(1)}, bf16[16,64,128]{2,1,0:T(8,128)(2,1)S(1)}, u32[]{:S(2)}, u32[]{:S(2)}) collective-permute-start(bf16[16,64,128]{2,1,0:T(8,128)(2,1)S(1)} %get-tuple-element.16), channel_id=1, source_target_pairs={{0,16},{8,24},{16,32},{24,40},{32,48},{40,56},{48,64},{56,72},{64,... | collective-permute-start | bytes 786440 | tf_op jit(solution)/shard_map/ppermute | solution.py:271
  17.7 19.7 %collective-permute-start.2 = (bf16[16,64,128]{2,1,0:T(8,128)(2,1)S(1)}, bf16[16,64,128]{2,1,0:T(8,128)(2,1)S(1)}, u32[]{:S(2)}, u32[]{:S(2)}) collective-permute-start(bf16[16,64,128]{2,1,0:T(8,128)(2,1)S(1)} %get-tuple-element.17), channel_id=1, source_target_pairs={{0,488},{8,480},{16,504},{24,496},{32,8},{40,0},{48,24},{56,16},{6... | collective-permute-start | bytes 786440 | tf_op jit(solution)/shard_map/ppermute | solution.py:271
  21.9 11.2 %collective-permute-start.3 = (bf16[16,64,128]{2,1,0:T(8,128)(2,1)S(1)}, bf16[16,64,128]{2,1,0:T(8,128)(2,1)S(1)}, u32[]{:S(2)}, u32[]{:S(2)}) collective-permute-start(bf16[16,64,128]{2,1,0:T(8,128)(2,1)S(1)} %get-tuple-element.18), channel_id=1, source_target_pairs={{0,24},{8,16},{16,40},{24,32},{32,56},{40,48},{48,72},{56,64},{64,... | collective-permute-start | bytes 786440 | tf_op jit(solution)/shard_map/ppermute | solution.py:271
  25.9 7.3 %collective-permute-start.4 = (bf16[16,64,128]{2,1,0:T(8,128)(2,1)S(1)}, bf16[16,64,128]{2,1,0:T(8,128)(2,1)S(1)}, u32[]{:S(2)}, u32[]{:S(2)}) collective-permute-start(bf16[16,64,128]{2,1,0:T(8,128)(2,1)S(1)} %get-tuple-element.20), channel_id=1, source_target_pairs={{0,8},{8,0},{16,24},{24,16},{32,40},{40,32},{48,56},{56,48},{64,72... | collective-permute-start | bytes 786440 | tf_op jit(solution)/shard_map/ppermute | solution.py:271
  54.3 4.5 %collective-permute-start.5 = (f32[2,16,128]{2,1,0:T(8,128)S(1)}, f32[2,16,128]{2,1,0:T(8,128)S(1)}, u32[]{:S(2)}, u32[]{:S(2)}) collective-permute-start(f32[2,16,128]{2,1,0:T(8,128)S(1)} %get-tuple-element.24), channel_id=1, source_target_pairs={{0,496},{8,504},{16,0},{24,8},{32,16},{40,24},{48,32},{56,40},{64,... | collective-permute-start | bytes 49160 | tf_op jit(solution)/shard_map/ppermute | solution.py:271

commit v8 on v6

--- a/solution.py
+++ b/solution.py
@@ -174,7 +174,7 @@
             for number in range(2):
                 for parity in range(2):
                     cut = slice(number * 16 + parity * 8, number * 16 + parity * 8 + 8)
-                    out_ref[parity * 8 + first_q + step, (2 if late else 0) + number] = (
+                    out_ref[(first_q + step) * 2 + parity, (2 if late else 0) + number] = (
                         jnp.concatenate([sums[0][cut], sums[1][cut]], axis=0).astype(
                             jnp.bfloat16
                         )
@@ -263,7 +263,7 @@
 def exchange(value):
     bands = lax.axis_size("band")
     groups = [
-        [(2 * chip + core) * bands + band for core in range(2) for band in range(bands)]
+        [(2 * chip + core) * bands + band for band in range(bands) for core in range(2)]
         for chip in range(lax.axis_size("pair") // 2)
     ]
     return lax.all_to_all(

time: 59.9 us -> 60.3 us (level)
  no operation moved by 1% of the time
where the time goes in v8:
time: 60.3 us; the launch traced here: 60 us
  starting transfers between devices  29.9 us (50%)
  blocking collectives  16.1 us (27%)
  waiting for transfers between devices  8.08 us (13%)
  Pallas kernels  5.5 us (9%)
    ppermute x6, starting transfers between devices, send(): return lax.ppermute(value, 'pair', pairs)  29.9 us
    all_to_all x1, blocking collectives, exchange(): lax.all_to_all(value, ('pair', 'band'), 0, 0, tiled=True, axis_index_grou...  16.1 us
    ppermute x6, waiting for transfers between devices, send(): return lax.ppermute(value, 'pair', pairs)  8.08 us
    pallas_call x2, Pallas kernels, cross(): pl.pallas_call(lambda *refs: cross_kernel(places, *refs), out_shape=shape...  3.1 us
    pallas_call x1, Pallas kernels, whiten(): pl.pallas_call(whiten_kernel, out_shape=(piece,) * 6, in_specs=[pl.BlockS...  1.73 us
  transfers between devices with their start and end apart: 6, of which 3 were waited for; matrix products, arithmetic and copies ran while one was open for 1% of the time, Pallas kernels for 3%

profile of v8, /device:TPU:1, one launch (start us, length us, event | category | flops | bytes accessed | tf_op | source)
XLA Modules:
  0.0 60.0 jit_solution(14704445678418226828)
XLA Ops:
  0.0 1.7 %shard_map.28 = (bf16[16,64,128]{2,1,0:T(8,128)(2,1)S(1)}, bf16[16,64,128]{2,1,0:T(8,128)(2,1)S(1)}, bf16[16,64,128]{2,1,0:T(8,128)(2,1)S(1)}, bf16[16,64,128]{2...) custom-call(bf16[2,64,8,256]{3,2,1,0:T(8,128)(2,1)} %spectra_hbm.1, ...), custom_call_target="tpu_custom_call" | custom-call | tf_op jit(solution)/shard_map/pallas_call | solution.py:73
  1.7 13.3 %collective-permute-start = (bf16[16,64,128]{2,1,0:T(8,128)(2,1)S(1)}, bf16[16,64,128]{2,1,0:T(8,128)(2,1)S(1)}, u32[]{:S(2)}, u32[]{:S(2)}) collective-permute-start(bf16[16,64,128]{2,1,0:T(8,128)(2,1)S(1)} %get-tuple-element.15), channel_id=1, source_target_pairs={{0,480},{8,488},{16,496},{24,504},{32,0},{40,8},{48,16},{56,24},{6... | collective-permute-start | bytes 786440 | tf_op jit(solution)/shard_map/ppermute | solution.py:260
  15.1 2.6 %collective-permute-start.1 = (bf16[16,64,128]{2,1,0:T(8,128)(2,1)S(1)}, bf16[16,64,128]{2,1,0:T(8,128)(2,1)S(1)}, u32[]{:S(2)}, u32[]{:S(2)}) collective-permute-start(bf16[16,64,128]{2,1,0:T(8,128)(2,1)S(1)} %get-tuple-element.16), channel_id=1, source_target_pairs={{0,16},{8,24},{16,32},{24,40},{32,48},{40,56},{48,64},{56,72},{64,... | collective-permute-start | bytes 786440 | tf_op jit(solution)/shard_map/ppermute | solution.py:260
  17.7 4.2 %collective-permute-start.2 = (bf16[16,64,128]{2,1,0:T(8,128)(2,1)S(1)}, bf16[16,64,128]{2,1,0:T(8,128)(2,1)S(1)}, u32[]{:S(2)}, u32[]{:S(2)}) collective-permute-start(bf16[16,64,128]{2,1,0:T(8,128)(2,1)S(1)} %get-tuple-element.17), channel_id=1, source_target_pairs={{0,488},{8,480},{16,504},{24,496},{32,8},{40,0},{48,24},{56,16},{6... | collective-permute-start | bytes 786440 | tf_op jit(solution)/shard_map/ppermute | solution.py:260
  21.9 3.9 %collective-permute-start.3 = (bf16[16,64,128]{2,1,0:T(8,128)(2,1)S(1)}, bf16[16,64,128]{2,1,0:T(8,128)(2,1)S(1)}, u32[]{:S(2)}, u32[]{:S(2)}) collective-permute-start(bf16[16,64,128]{2,1,0:T(8,128)(2,1)S(1)} %get-tuple-element.18), channel_id=1, source_target_pairs={{0,24},{8,16},{16,40},{24,32},{32,56},{40,48},{48,72},{56,64},{64,... | collective-permute-start | bytes 786440 | tf_op jit(solution)/shard_map/ppermute | solution.py:260
  25.9 3.1 %collective-permute-start.4 = (bf16[16,64,128]{2,1,0:T(8,128)(2,1)S(1)}, bf16[16,64,128]{2,1,0:T(8,128)(2,1)S(1)}, u32[]{:S(2)}, u32[]{:S(2)}) collective-permute-start(bf16[16,64,128]{2,1,0:T(8,128)(2,1)S(1)} %get-tuple-element.20), channel_id=1, source_target_pairs={{0,8},{8,0},{16,24},{24,16},{32,40},{40,32},{48,56},{56,48},{64,72... | collective-permute-start | bytes 786440 | tf_op jit(solution)/shard_map/ppermute | solution.py:260
  29.0 0.3 fusion.3
  29.4 0.0 collective-permute-done.1.refs_0_.refs_1_
  29.4 3.7 %collective-permute-done.3.refs_1_ = bf16[16,64,128]{2,1,0:T(8,128)(2,1)S(1)} collective-permute-done((bf16[16,64,128]{2,1,0:T(8,128)(2,1)S(1)}, bf16[16,64,128]{2,1,0:T(8,128)(2,1)S(1)}, u32[]{:S(2)}, u32[]{:S(2)}) %collective-permute-start.3) | collective-permute-done | bytes 262176 | tf_op jit(solution)/shard_map/ppermute | solution.py:260
  33.1 0.0 collective-permute-done.4.refs_3_
  33.1 1.8 %shard_map.29 = (bf16[16,2,16,128]{3,2,1,0:T(8,128)(2,1)S(1)}, bf16[2,16,256,128]{3,2,1,0:T(8,128)(2,1)S(1)}) custom-call(bf16[16,64,128]{2,1,0:T(8,128)(2,1)S(1)} %collective-permute-done.1.refs_0_.refs_1_, bf16[16,64,128]{2,1,0:T(8,128)(2,1)S(1)} %collective-permute-done.3.refs_1_, bf16[16,64,128]{2,1,0:T(8,128)(2,1)S(1)} %get-tuple-element.19.refs_2_, ...), custom_call_target="tpu_custom_call" | custom-call | flops 402653184 | bytes 1310720 | tf_op jit(solution)/shard_map/pallas_call | solution.py:188
  34.9 0.0 collective-permute-done.refs_0_
  34.9 2.5 %collective-permute-done.2.refs_2_ = bf16[16,64,128]{2,1,0:T(8,128)(2,1)S(1)} collective-permute-done((bf16[16,64,128]{2,1,0:T(8,128)(2,1)S(1)}, bf16[16,64,128]{2,1,0:T(8,128)(2,1)S(1)}, u32[]{:S(2)}, u32[]{:S(2)}) %collective-permute-start.2) | collective-permute-done | bytes 262176 | tf_op jit(solution)/shard_map/ppermute | solution.py:260
  37.4 1.3 %shard_map.30 = bf16[16,4,16,128]{3,2,1,0:T(8,128)(2,1)S(1)} custom-call(bf16[16,64,128]{2,1,0:T(8,128)(2,1)S(1)} %collective-permute-done.refs_0_, bf16[16,64,128]{2,1,0:T(8,128)(2,1)S(1)} %collective-permute-done.1.refs_0_.refs_1_, bf16[16,64,128]{2,1,0:T(8,128)(2,1)S(1)} %collective-permute-done.2.refs_2_, ...), custom_call_target="tpu_custom_call" | custom-call | flops 402653184 | bytes 1048576 | tf_op jit(solution)/shard_map/pallas_call | solution.py:188
  38.8 16.1 %all_to_all.5.parts_ref = bf16[16,4,16,128]{3,2,1,0:T(8,128)(2,1)S(1)} all-to-all(bf16[16,4,16,128]{3,2,1,0:T(8,128)(2,1)S(1)} %shard_map.30), channel_id=1, replica_groups={{0,8,1,9,2,10,3,11,4,12,5,13,6,14,7,15},{16,24,17,25,18,26,19,27,20,28,..., dimensions={0} | all-to-all | bytes 524288 | tf_op jit(solution)/shard_map/all_to_all | solution.py:269
  54.9 2.7 %collective-permute-start.5 = (f32[2,16,128]{2,1,0:T(8,128)S(1)}, f32[2,16,128]{2,1,0:T(8,128)S(1)}, u32[]{:S(2)}, u32[]{:S(2)}) collective-permute-start(f32[2,16,128]{2,1,0:T(8,128)S(1)} %get-tuple-element.24), channel_id=1, source_target_pairs={{0,496},{8,504},{16,0},{24,8},{32,16},{40,24},{48,32},{56,40},{64,... | collective-permute-start | bytes 49160 | tf_op jit(solution)/shard_map/ppermute | solution.py:260
  57.6 1.8 %collective-permute-done.5.away_ref = f32[2,16,128]{2,1,0:T(8,128)S(1)} collective-permute-done((f32[2,16,128]{2,1,0:T(8,128)S(1)}, f32[2,16,128]{2,1,0:T(8,128)S(1)}, u32[]{:S(2)}, u32[]{:S(2)}) %collective-permute-start.5) | collective-permute-done | bytes 16416 | tf_op jit(solution)/shard_map/ppermute | solution.py:260
  59.4 0.6 %shard_map.32 = f32[7,8,128]{2,1,0:T(8,128)} custom-call(f32[2,16,128]{2,1,0:T(8,128)S(1)} %get-tuple-element.23.home_ref, f32[2,16,128]{2,1,0:T(8,128)S(1)} %collective-permute-done.5.away_ref), custom_call_target="tpu_custom_call" | custom-call | tf_op jit(solution)/shard_map/pallas_call | solution.py:244
  (3 shorter events, 0.1 us)
Async XLA Ops:
  1.7 33.2 %collective-permute-start = (bf16[16,64,128]{2,1,0:T(8,128)(2,1)S(1)}, bf16[16,64,128]{2,1,0:T(8,128)(2,1)S(1)}, u32[]{:S(2)}, u32[]{:S(2)}) collective-permute-start(bf16[16,64,128]{2,1,0:T(8,128)(2,1)S(1)} %get-tuple-element.15), channel_id=1, source_target_pairs={{0,480},{8,488},{16,496},{24,504},{32,0},{40,8},{48,16},{56,24},{6... | collective-permute-start | bytes 786440 | tf_op jit(solution)/shard_map/ppermute | solution.py:260
  15.1 14.3 %collective-permute-start.1 = (bf16[16,64,128]{2,1,0:T(8,128)(2,1)S(1)}, bf16[16,64,128]{2,1,0:T(8,128)(2,1)S(1)}, u32[]{:S(2)}, u32[]{:S(2)}) collective-permute-start(bf16[16,64,128]{2,1,0:T(8,128)(2,1)S(1)} %get-tuple-element.16), channel_id=1, source_target_pairs={{0,16},{8,24},{16,32},{24,40},{32,48},{40,56},{48,64},{56,72},{64,... | collective-permute-start | bytes 786440 | tf_op jit(solution)/shard_map/ppermute | solution.py:260
  17.7 19.7 %collective-permute-start.2 = (bf16[16,64,128]{2,1,0:T(8,128)(2,1)S(1)}, bf16[16,64,128]{2,1,0:T(8,128)(2,1)S(1)}, u32[]{:S(2)}, u32[]{:S(2)}) collective-permute-start(bf16[16,64,128]{2,1,0:T(8,128)(2,1)S(1)} %get-tuple-element.17), channel_id=1, source_target_pairs={{0,488},{8,480},{16,504},{24,496},{32,8},{40,0},{48,24},{56,16},{6... | collective-permute-start | bytes 786440 | tf_op jit(solution)/shard_map/ppermute | solution.py:260
  21.9 11.2 %collective-permute-start.3 = (bf16[16,64,128]{2,1,0:T(8,128)(2,1)S(1)}, bf16[16,64,128]{2,1,0:T(8,128)(2,1)S(1)}, u32[]{:S(2)}, u32[]{:S(2)}) collective-permute-start(bf16[16,64,128]{2,1,0:T(8,128)(2,1)S(1)} %get-tuple-element.18), channel_id=1, source_target_pairs={{0,24},{8,16},{16,40},{24,32},{32,56},{40,48},{48,72},{56,64},{64,... | collective-permute-start | bytes 786440 | tf_op jit(solution)/shard_map/ppermute | solution.py:260
  25.9 7.3 %collective-permute-start.4 = (bf16[16,64,128]{2,1,0:T(8,128)(2,1)S(1)}, bf16[16,64,128]{2,1,0:T(8,128)(2,1)S(1)}, u32[]{:S(2)}, u32[]{:S(2)}) collective-permute-start(bf16[16,64,128]{2,1,0:T(8,128)(2,1)S(1)} %get-tuple-element.20), channel_id=1, source_target_pairs={{0,8},{8,0},{16,24},{24,16},{32,40},{40,32},{48,56},{56,48},{64,72... | collective-permute-start | bytes 786440 | tf_op jit(solution)/shard_map/ppermute | solution.py:260
  54.9 4.5 %collective-permute-start.5 = (f32[2,16,128]{2,1,0:T(8,128)S(1)}, f32[2,16,128]{2,1,0:T(8,128)S(1)}, u32[]{:S(2)}, u32[]{:S(2)}) collective-permute-start(f32[2,16,128]{2,1,0:T(8,128)S(1)} %get-tuple-element.24), channel_id=1, source_target_pairs={{0,496},{8,504},{16,0},{24,8},{32,16},{40,24},{48,32},{56,40},{64,... | collective-permute-start | bytes 49160 | tf_op jit(solution)/shard_map/ppermute | solution.py:260
